TPU v7x, 256 devices: a whole 4x4x8 slice. The times are simulated.
256 devices in a mesh: dx: 16 (over x, z_lo), dy: 16 (over z_hi, y, core).
Axes of the slice: x: 4, y: 4, z: 8 (z_hi: 2, z_lo: 4; z = z_hi * 4 + z_lo), core: 2. Of those that a mesh axis runs over, the one named last changes fastest.
Arguments:
- queries: bfloat16 [98304, 1024], P(('dx', 'dy')), may hold values from -1.25 to 1.25
- documents: bfloat16 [98304, 1024], P(('dx', 'dy')), may hold values from -8 to 10
- positives: int32 [98304], P(('dx', 'dy')), may hold values from 0 to 98303, as said below
Outputs:
- row_loss: float32 [98304], P(('dx', 'dy'))
- grad_queries: float32 [98304, 1024], P(('dx', 'dy'))
- grad_documents: float32 [98304, 1024], P(('dx', 'dy'))
Inputs may be any that keep to these rules, and one draw needn't show every extreme that they name: positives[i] lies in the block of 384 rows that holds row i, and within each block every row is the positive of exactly one query.
All inputs are finite; a program needn't handle non-finite values.
Results may differ from a plain program's by a relative error of at most 0.0028.
Values may be sent and summed in bfloat16 or wider, within the bound.
A program may use at most 64 MiB of HBM per device.

v0:
```python
import jax
import jax.numpy as jnp
from jax import lax
from jax.sharding import PartitionSpec as P

LOGIT_SCALE = 20.0


def shifted(block, axis, distance):
    devices = range(lax.axis_size(axis))
    route = [((i - distance) % len(devices), i) for i in devices]
    return lax.ppermute(block, axis, route)


def make_tile(left, right):
    return LOGIT_SCALE * lax.dot_general(
        left, right, (((1,), (1,)), ((), ())), preferred_element_type=jnp.float32
    )


def log_total(scores, axis):
    return jax.nn.logsumexp(scores, axis=axis)


def tile_weights(scores, row_part, col_part):
    return (
        0.5 * (jnp.exp(scores - row_part[:, None]) + jnp.exp(scores - col_part[None, :]))
    ).astype(jnp.bfloat16)


def row_product(weight, right):
    return LOGIT_SCALE * jnp.dot(weight, right, preferred_element_type=jnp.float32)


def col_product(weight, left):
    return LOGIT_SCALE * lax.dot_general(
        weight, left, (((0,), (0,)), ((), ())), preferred_element_type=jnp.float32
    )


def per_device(queries, documents, positives):
    row_count = queries.shape[0]
    stride = lax.axis_size("dy") + 1
    rounds = min(4, (lax.axis_size("dx") * lax.axis_size("dy") - 1) // (2 * stride))
    local_pos = jnp.remainder(positives, row_count)
    own_tile = make_tile(queries, documents)
    matches = lax.broadcasted_iota(jnp.int32, (row_count, row_count), 1) == local_pos[:, None]
    row_lse = log_total(own_tile, 1)
    col_lse = log_total(own_tile, 0)
    kept = []
    for round_index in range(1, rounds + 1):
        offset = round_index * stride
        lower_queries, lower_docs = shifted((queries, documents), ("dx", "dy"), offset)
        lower_tile = make_tile(queries, lower_docs)
        mirror_tile = make_tile(lower_queries, documents)
        row_lse = jnp.logaddexp(row_lse, log_total(lower_tile, 1))
        col_lse = jnp.logaddexp(col_lse, log_total(mirror_tile, 0))
        got_rows, got_cols = shifted(
            (log_total(mirror_tile, 1), log_total(lower_tile, 0)), ("dx", "dy"), -offset
        )
        row_lse = jnp.logaddexp(row_lse, got_rows)
        col_lse = jnp.logaddexp(col_lse, got_cols)
        kept.append((lower_queries, lower_docs, lower_tile, mirror_tile))
    positive_score = jnp.sum(jnp.where(matches, own_tile, 0.0), axis=1)
    col_at_pos = jnp.sum(jnp.where(matches, col_lse[None, :], 0.0), axis=1)
    row_loss = 0.5 * (row_lse - positive_score) + 0.5 * (col_at_pos - positive_score)
    own_weight = (
        0.5 * (jnp.exp(own_tile - row_lse[:, None]) + jnp.exp(own_tile - col_lse[None, :]))
        - matches.astype(jnp.float32)
    ).astype(jnp.bfloat16)
    grad_queries = row_product(own_weight, documents)
    grad_documents = col_product(own_weight, queries)
    for round_index, saved in enumerate(kept):
        offset = (round_index + 1) * stride
        lower_rows, lower_cols = shifted((row_lse, col_lse), ("dx", "dy"), offset)
        lower_queries, lower_docs, lower_tile, mirror_tile = saved[:4]
        lower_weight = tile_weights(lower_tile, row_lse, lower_cols)
        mirror_weight = tile_weights(mirror_tile, lower_rows, col_lse)
        grad_queries = grad_queries + row_product(lower_weight, lower_docs)
        grad_documents = grad_documents + col_product(mirror_weight, lower_queries)
        back_queries = row_product(mirror_weight, documents)
        back_docs = col_product(lower_weight, queries)
        got_queries, got_docs = (
            shifted(back_queries.astype(jnp.bfloat16), ("dx", "dy"), -offset).astype(
                back_queries.dtype
            ),
            shifted(back_docs.astype(jnp.bfloat16), ("dx", "dy"), -offset).astype(back_docs.dtype),
        )
        grad_queries = grad_queries + got_queries
        grad_documents = grad_documents + got_docs
    return (row_loss, grad_queries, grad_documents)


def solution(mesh):
    return jax.shard_map(
        per_device,
        mesh=mesh,
        in_specs=(P(("dx", "dy"), None), P(("dx", "dy"), None), P(("dx", "dy"))),
        out_specs=(P(("dx", "dy")), P(("dx", "dy"), None), P(("dx", "dy"), None)),
        check_vma=False,
    )
```

profile of v0, /device:TPU:6, one launch (start us, length us, event | category | flops | bytes accessed | tf_op | source)
XLA Modules:
  0.0 592.3 jit_solution(1227920626357272147)
XLA Ops:
  0.6 1.4 collective-permute-start
  2.1 4.3 collective-permute-start.3
  6.4 2.7 collective-permute-start.6
  9.0 5.8 collective-permute-start.9
  14.8 2.0 fusion.21
  17.2 70.6 %collective-permute-done = bf16[384,1024]{1,0:T(8,128)(2,1)S(1)} collective-permute-done((bf16[384,1024]{1,0:T(8,128)(2,1)}, bf16[384,1024]{1,0:T(8,128)(2,1)S(1)}, u32[]{:S(2)}, u32[]{:S(2)}) %collective-permute-start) | collective-permute-done | bytes 786464 | tf_op jit(solution)/shard_map/ppermute | solution.py:12
  88.5 27.7 %collective-permute-start.7 = (bf16[384,1024]{1,0:T(8,128)(2,1)S(1)}, bf16[384,1024]{1,0:T(8,128)(2,1)S(1)}, u32[]{:S(2)}, u32[]{:S(2)}) collective-permute-start(bf16[384,1024]{1,0:T(8,128)(2,1)S(1)} %copy-done), channel_id=1, source_target_pairs={{205,0},{206,1},{207,2},{208,3},{209,4},{210,5},{211,6},{212,7},{2... | collective-permute-start | bytes 2359304 | tf_op jit(solution)/shard_map/ppermute | solution.py:12
  117.0 39.5 %collective-permute-start.10 = (bf16[384,1024]{1,0:T(8,128)(2,1)S(1)}, bf16[384,1024]{1,0:T(8,128)(2,1)S(1)}, u32[]{:S(2)}, u32[]{:S(2)}) collective-permute-start(bf16[384,1024]{1,0:T(8,128)(2,1)S(1)} %copy-done), channel_id=1, source_target_pairs={{188,0},{189,1},{190,2},{191,3},{192,4},{193,5},{194,6},{195,7},{1... | collective-permute-start | bytes 2359304 | tf_op jit(solution)/shard_map/ppermute | solution.py:12
  159.1 15.0 %collective-permute-done.1 = bf16[384,1024]{1,0:T(8,128)(2,1)S(1)} collective-permute-done((bf16[384,1024]{1,0:T(8,128)(2,1)}, bf16[384,1024]{1,0:T(8,128)(2,1)S(1)}, u32[]{:S(2)}, u32[]{:S(2)}) %collective-permute-start.1) | collective-permute-done | bytes 786464 | tf_op jit(solution)/shard_map/ppermute | solution.py:12
  177.8 36.1 %collective-permute-start.2 = (f32[384]{0:T(512)S(1)}, f32[384]{0:T(512)S(1)}, u32[]{:S(2)}, u32[]{:S(2)}) collective-permute-start(f32[384]{0:T(512)S(1)} %log_add_fusion.15), channel_id=1, source_target_pairs={{17,0},{18,1},{19,2},{20,3},{21,4},{22,5},{23,6},{24,7},{25,8},{26... | collective-permute-start | bytes 4616 | tf_op jit(solution)/shard_map/ppermute | solution.py:12
  215.1 12.2 %collective-permute-done.14 = f32[384]{0:T(512)S(1)} collective-permute-done((f32[384]{0:T(512)S(1)}, f32[384]{0:T(512)S(1)}, u32[]{:S(2)}, u32[]{:S(2)}) %collective-permute-start.14) | collective-permute-done | bytes 1568 | tf_op jit(solution)/shard_map/ppermute | solution.py:12
  227.3 4.8 collective-permute-start.11
  233.4 27.9 %collective-permute-done.11 = f32[384]{0:T(512)S(1)} collective-permute-done((f32[384]{0:T(512)S(1)}, f32[384]{0:T(512)S(1)}, u32[]{:S(2)}, u32[]{:S(2)}) %collective-permute-start.11) | collective-permute-done | bytes 1568 | tf_op jit(solution)/shard_map/ppermute | solution.py:12
  262.1 6.8 %collective-permute-start.20 = (f32[384]{0:T(512)S(1)}, f32[384]{0:T(512)S(1)}, u32[]{:S(2)}, u32[]{:S(2)}) collective-permute-start(f32[384]{0:T(512)S(1)} %get-tuple-element.41), channel_id=1, source_target_pairs={{222,0},{223,1},{224,2},{225,3},{226,4},{227,5},{228,6},{229,7},{2... | collective-permute-start | bytes 4616 | tf_op jit(solution)/shard_map/ppermute | solution.py:12
  268.9 9.1 %collective-permute-start.23 = (f32[384]{0:T(512)S(1)}, f32[384]{0:T(512)S(1)}, u32[]{:S(2)}, u32[]{:S(2)}) collective-permute-start(f32[384]{0:T(512)S(1)} %get-tuple-element.41), channel_id=1, source_target_pairs={{205,0},{206,1},{207,2},{208,3},{209,4},{210,5},{211,6},{212,7},{2... | collective-permute-start | bytes 4616 | tf_op jit(solution)/shard_map/ppermute | solution.py:12
  278.0 6.3 %collective-permute-start.26 = (f32[384]{0:T(512)S(1)}, f32[384]{0:T(512)S(1)}, u32[]{:S(2)}, u32[]{:S(2)}) collective-permute-start(f32[384]{0:T(512)S(1)} %get-tuple-element.41), channel_id=1, source_target_pairs={{188,0},{189,1},{190,2},{191,3},{192,4},{193,5},{194,6},{195,7},{1... | collective-permute-start | bytes 4616 | tf_op jit(solution)/shard_map/ppermute | solution.py:12
  284.3 1.9 collective-permute-start.16
  286.2 7.8 %collective-permute-start.19 = (f32[384]{0:T(512)S(1)}, f32[384]{0:T(512)S(1)}, u32[]{:S(2)}, u32[]{:S(2)}) collective-permute-start(f32[384]{0:T(512)S(1)} %add_select_fusion.1), channel_id=1, source_target_pairs={{222,0},{223,1},{224,2},{225,3},{226,4},{227,5},{228,6},{229,7},{2... | collective-permute-start | bytes 4616 | tf_op jit(solution)/shard_map/ppermute | solution.py:12
  295.5 3.6 collective-permute-start.22
  299.8 4.5 collective-permute-start.25
  305.6 7.8 %collective-permute-start.17 = (f32[384]{0:T(512)S(1)}, f32[384]{0:T(512)S(1)}, u32[]{:S(2)}, u32[]{:S(2)}) collective-permute-start(f32[384]{0:T(512)S(1)} %get-tuple-element.41), channel_id=1, source_target_pairs={{239,0},{240,1},{241,2},{242,3},{243,4},{244,5},{245,6},{246,7},{2... | collective-permute-start | bytes 4616 | tf_op jit(solution)/shard_map/ppermute | solution.py:12
  315.6 1.0 collective-permute-start.29
  317.2 3.7 collective-permute-start.30
  322.3 14.4 %collective-permute-start.18 = (bf16[384,1024]{1,0:T(8,128)(2,1)S(1)}, bf16[384,1024]{1,0:T(8,128)(2,1)S(1)}, u32[]{:S(2)}, u32[]{:S(2)}) collective-permute-start(bf16[384,1024]{1,0:T(8,128)(2,1)S(1)} %multiply_convert_fusion.7), channel_id=1, source_target_pairs={{17,0},{18,1},{19,2},{20,3},{21,4},{22,5},{23,6},{24,7},{25,8},{26... | collective-permute-start | bytes 2359304 | tf_op jit(solution)/shard_map/ppermute | solution.py:12
  339.6 163.2 %collective-permute-done.28 = bf16[384,1024]{1,0:T(8,128)(2,1)S(1)} collective-permute-done((bf16[384,1024]{1,0:T(8,128)(2,1)S(1)}, bf16[384,1024]{1,0:T(8,128)(2,1)S(1)}, u32[]{:S(2)}, u32[]{:S(2)}) %collective-permute-start.28) | collective-permute-done | bytes 786464 | tf_op jit(solution)/shard_map/ppermute | solution.py:12
  502.8 32.5 %collective-permute-done.29 = bf16[384,1024]{1,0:T(8,128)(2,1)S(1)} collective-permute-done((bf16[384,1024]{1,0:T(8,128)(2,1)S(1)}, bf16[384,1024]{1,0:T(8,128)(2,1)S(1)}, u32[]{:S(2)}, u32[]{:S(2)}) %collective-permute-start.29) | collective-permute-done | bytes 786464 | tf_op jit(solution)/shard_map/ppermute | solution.py:12
  536.0 24.5 %collective-permute-done.31 = bf16[384,1024]{1,0:T(8,128)(2,1)S(1)} collective-permute-done((bf16[384,1024]{1,0:T(8,128)(2,1)S(1)}, bf16[384,1024]{1,0:T(8,128)(2,1)S(1)}, u32[]{:S(2)}, u32[]{:S(2)}) %collective-permute-start.31) | collective-permute-done | bytes 786464 | tf_op jit(solution)/shard_map/ppermute | solution.py:12
  560.5 2.4 fusion.5
  563.0 9.8 %collective-permute-done.18 = bf16[384,1024]{1,0:T(8,128)(2,1)S(1)} collective-permute-done((bf16[384,1024]{1,0:T(8,128)(2,1)S(1)}, bf16[384,1024]{1,0:T(8,128)(2,1)S(1)}, u32[]{:S(2)}, u32[]{:S(2)}) %collective-permute-start.18) | collective-permute-done | bytes 786464 | tf_op jit(solution)/shard_map/ppermute | solution.py:12
  572.7 8.4 %collective-permute-done.21 = bf16[384,1024]{1,0:T(8,128)(2,1)S(1)} collective-permute-done((bf16[384,1024]{1,0:T(8,128)(2,1)S(1)}, bf16[384,1024]{1,0:T(8,128)(2,1)S(1)}, u32[]{:S(2)}, u32[]{:S(2)}) %collective-permute-start.21) | collective-permute-done | bytes 786464 | tf_op jit(solution)/shard_map/ppermute | solution.py:12
  581.2 8.4 %collective-permute-done.27 = bf16[384,1024]{1,0:T(8,128)(2,1)S(1)} collective-permute-done((bf16[384,1024]{1,0:T(8,128)(2,1)S(1)}, bf16[384,1024]{1,0:T(8,128)(2,1)S(1)}, u32[]{:S(2)}, u32[]{:S(2)}) %collective-permute-start.27) | collective-permute-done | bytes 786464 | tf_op jit(solution)/shard_map/ppermute | solution.py:12
  589.6 2.5 fusion.11
  (95 shorter events, 22.2 us)
Async XLA Ops:
  0.6 87.2 %collective-permute-start = (bf16[384,1024]{1,0:T(8,128)(2,1)}, bf16[384,1024]{1,0:T(8,128)(2,1)S(1)}, u32[]{:S(2)}, u32[]{:S(2)}) collective-permute-start(bf16[384,1024]{1,0:T(8,128)(2,1)} %param.4), channel_id=1, source_target_pairs={{239,0},{240,1},{241,2},{242,3},{243,4},{244,5},{245,6},{246,7},{2... | collective-permute-start | bytes 2359304 | tf_op jit(solution)/shard_map/ppermute | solution.py:12
  2.1 86.4 %collective-permute-start.3 = (bf16[384,1024]{1,0:T(8,128)(2,1)}, bf16[384,1024]{1,0:T(8,128)(2,1)S(1)}, u32[]{:S(2)}, u32[]{:S(2)}) collective-permute-start(bf16[384,1024]{1,0:T(8,128)(2,1)} %param.4), channel_id=1, source_target_pairs={{222,0},{223,1},{224,2},{225,3},{226,4},{227,5},{228,6},{229,7},{2... | collective-permute-start | bytes 2359304 | tf_op jit(solution)/shard_map/ppermute | solution.py:12
  6.4 110.6 %collective-permute-start.6 = (bf16[384,1024]{1,0:T(8,128)(2,1)}, bf16[384,1024]{1,0:T(8,128)(2,1)S(1)}, u32[]{:S(2)}, u32[]{:S(2)}) collective-permute-start(bf16[384,1024]{1,0:T(8,128)(2,1)} %param.4), channel_id=1, source_target_pairs={{205,0},{206,1},{207,2},{208,3},{209,4},{210,5},{211,6},{212,7},{2... | collective-permute-start | bytes 2359304 | tf_op jit(solution)/shard_map/ppermute | solution.py:12
  9.0 149.0 %collective-permute-start.9 = (bf16[384,1024]{1,0:T(8,128)(2,1)}, bf16[384,1024]{1,0:T(8,128)(2,1)S(1)}, u32[]{:S(2)}, u32[]{:S(2)}) collective-permute-start(bf16[384,1024]{1,0:T(8,128)(2,1)} %param.4), channel_id=1, source_target_pairs={{188,0},{189,1},{190,2},{191,3},{192,4},{193,5},{194,6},{195,7},{1... | collective-permute-start | bytes 2359304 | tf_op jit(solution)/shard_map/ppermute | solution.py:12
  14.8 159.3 %collective-permute-start.1 = (bf16[384,1024]{1,0:T(8,128)(2,1)}, bf16[384,1024]{1,0:T(8,128)(2,1)S(1)}, u32[]{:S(2)}, u32[]{:S(2)}) collective-permute-start(bf16[384,1024]{1,0:T(8,128)(2,1)} %param.3), channel_id=1, source_target_pairs={{239,0},{240,1},{241,2},{242,3},{243,4},{244,5},{245,6},{246,7},{2... | collective-permute-start | bytes 2359304 | tf_op jit(solution)/shard_map/ppermute | solution.py:12
  87.8 87.0 %collective-permute-start.4 = (bf16[384,1024]{1,0:T(8,128)(2,1)S(1)}, bf16[384,1024]{1,0:T(8,128)(2,1)S(1)}, u32[]{:S(2)}, u32[]{:S(2)}) collective-permute-start(bf16[384,1024]{1,0:T(8,128)(2,1)S(1)} %copy-done), channel_id=1, source_target_pairs={{222,0},{223,1},{224,2},{225,3},{226,4},{227,5},{228,6},{229,7},{2... | collective-permute-start | bytes 2359304 | tf_op jit(solution)/shard_map/ppermute | solution.py:12
  88.5 87.6 %collective-permute-start.7 = (bf16[384,1024]{1,0:T(8,128)(2,1)S(1)}, bf16[384,1024]{1,0:T(8,128)(2,1)S(1)}, u32[]{:S(2)}, u32[]{:S(2)}) collective-permute-start(bf16[384,1024]{1,0:T(8,128)(2,1)S(1)} %copy-done), channel_id=1, source_target_pairs={{205,0},{206,1},{207,2},{208,3},{209,4},{210,5},{211,6},{212,7},{2... | collective-permute-start | bytes 2359304 | tf_op jit(solution)/shard_map/ppermute | solution.py:12
  117.0 60.8 %collective-permute-start.10 = (bf16[384,1024]{1,0:T(8,128)(2,1)S(1)}, bf16[384,1024]{1,0:T(8,128)(2,1)S(1)}, u32[]{:S(2)}, u32[]{:S(2)}) collective-permute-start(bf16[384,1024]{1,0:T(8,128)(2,1)S(1)} %copy-done), channel_id=1, source_target_pairs={{188,0},{189,1},{190,2},{191,3},{192,4},{193,5},{194,6},{195,7},{1... | collective-permute-start | bytes 2359304 | tf_op jit(solution)/shard_map/ppermute | solution.py:12
  158.1 56.8 %collective-permute-start.12 = (f32[384]{0:T(512)S(1)}, f32[384]{0:T(512)S(1)}, u32[]{:S(2)}, u32[]{:S(2)}) collective-permute-start(f32[384]{0:T(512)S(1)} %log_add_fusion.6), channel_id=1, source_target_pairs={{17,0},{18,1},{19,2},{20,3},{21,4},{22,5},{23,6},{24,7},{25,8},{26... | collective-permute-start | bytes 4616 | tf_op jit(solution)/shard_map/ppermute | solution.py:12
  174.1 40.8 %collective-permute-start.13 = (f32[384]{0:T(512)S(1)}, f32[384]{0:T(512)S(1)}, u32[]{:S(2)}, u32[]{:S(2)}) collective-permute-start(f32[384]{0:T(512)S(1)} %log_add_fusion.4), channel_id=1, source_target_pairs={{34,0},{35,1},{36,2},{37,3},{38,4},{39,5},{40,6},{41,7},{42,8},{43... | collective-permute-start | bytes 4616 | tf_op jit(solution)/shard_map/ppermute | solution.py:12
  174.8 52.5 %collective-permute-start.14 = (f32[384]{0:T(512)S(1)}, f32[384]{0:T(512)S(1)}, u32[]{:S(2)}, u32[]{:S(2)}) collective-permute-start(f32[384]{0:T(512)S(1)} %log_add_fusion.2), channel_id=1, source_target_pairs={{51,0},{52,1},{53,2},{54,3},{55,4},{56,5},{57,6},{58,7},{59,8},{60... | collective-permute-start | bytes 4616 | tf_op jit(solution)/shard_map/ppermute | solution.py:12
  176.1 56.5 %collective-permute-start.15 = (f32[384]{0:T(512)S(1)}, f32[384]{0:T(512)S(1)}, u32[]{:S(2)}, u32[]{:S(2)}) collective-permute-start(f32[384]{0:T(512)S(1)} %log_add_fusion), channel_id=1, source_target_pairs={{68,0},{69,1},{70,2},{71,3},{72,4},{73,5},{74,6},{75,7},{76,8},{77... | collective-permute-start | bytes 4616 | tf_op jit(solution)/shard_map/ppermute | solution.py:12
  177.8 55.1 %collective-permute-start.2 = (f32[384]{0:T(512)S(1)}, f32[384]{0:T(512)S(1)}, u32[]{:S(2)}, u32[]{:S(2)}) collective-permute-start(f32[384]{0:T(512)S(1)} %log_add_fusion.15), channel_id=1, source_target_pairs={{17,0},{18,1},{19,2},{20,3},{21,4},{22,5},{23,6},{24,7},{25,8},{26... | collective-permute-start | bytes 4616 | tf_op jit(solution)/shard_map/ppermute | solution.py:12
  214.9 18.0 %collective-permute-start.5 = (f32[384]{0:T(512)S(1)}, f32[384]{0:T(512)S(1)}, u32[]{:S(2)}, u32[]{:S(2)}) collective-permute-start(f32[384]{0:T(512)S(1)} %log_add_fusion.13), channel_id=1, source_target_pairs={{34,0},{35,1},{36,2},{37,3},{38,4},{39,5},{40,6},{41,7},{42,8},{43... | collective-permute-start | bytes 4616 | tf_op jit(solution)/shard_map/ppermute | solution.py:12
  215.0 18.4 %collective-permute-start.8 = (f32[384]{0:T(512)S(1)}, f32[384]{0:T(512)S(1)}, u32[]{:S(2)}, u32[]{:S(2)}) collective-permute-start(f32[384]{0:T(512)S(1)} %log_add_fusion.11), channel_id=1, source_target_pairs={{51,0},{52,1},{53,2},{54,3},{55,4},{56,5},{57,6},{58,7},{59,8},{60... | collective-permute-start | bytes 4616 | tf_op jit(solution)/shard_map/ppermute | solution.py:12
  227.3 34.0 %collective-permute-start.11 = (f32[384]{0:T(512)S(1)}, f32[384]{0:T(512)S(1)}, u32[]{:S(2)}, u32[]{:S(2)}) collective-permute-start(f32[384]{0:T(512)S(1)} %log_add_fusion.9), channel_id=1, source_target_pairs={{68,0},{69,1},{70,2},{71,3},{72,4},{73,5},{74,6},{75,7},{76,8},{77... | collective-permute-start | bytes 4616 | tf_op jit(solution)/shard_map/ppermute | solution.py:12
  262.1 33.4 %collective-permute-start.20 = (f32[384]{0:T(512)S(1)}, f32[384]{0:T(512)S(1)}, u32[]{:S(2)}, u32[]{:S(2)}) collective-permute-start(f32[384]{0:T(512)S(1)} %get-tuple-element.41), channel_id=1, source_target_pairs={{222,0},{223,1},{224,2},{225,3},{226,4},{227,5},{228,6},{229,7},{2... | collective-permute-start | bytes 4616 | tf_op jit(solution)/shard_map/ppermute | solution.py:12
  268.9 45.2 %collective-permute-start.23 = (f32[384]{0:T(512)S(1)}, f32[384]{0:T(512)S(1)}, u32[]{:S(2)}, u32[]{:S(2)}) collective-permute-start(f32[384]{0:T(512)S(1)} %get-tuple-element.41), channel_id=1, source_target_pairs={{205,0},{206,1},{207,2},{208,3},{209,4},{210,5},{211,6},{212,7},{2... | collective-permute-start | bytes 4616 | tf_op jit(solution)/shard_map/ppermute | solution.py:12
  278.0 44.3 %collective-permute-start.26 = (f32[384]{0:T(512)S(1)}, f32[384]{0:T(512)S(1)}, u32[]{:S(2)}, u32[]{:S(2)}) collective-permute-start(f32[384]{0:T(512)S(1)} %get-tuple-element.41), channel_id=1, source_target_pairs={{188,0},{189,1},{190,2},{191,3},{192,4},{193,5},{194,6},{195,7},{1... | collective-permute-start | bytes 4616 | tf_op jit(solution)/shard_map/ppermute | solution.py:12
  284.3 21.3 %collective-permute-start.16 = (f32[384]{0:T(512)S(1)}, f32[384]{0:T(512)S(1)}, u32[]{:S(2)}, u32[]{:S(2)}) collective-permute-start(f32[384]{0:T(512)S(1)} %add_select_fusion.1), channel_id=1, source_target_pairs={{239,0},{240,1},{241,2},{242,3},{243,4},{244,5},{245,6},{246,7},{2... | collective-permute-start | bytes 4616 | tf_op jit(solution)/shard_map/ppermute | solution.py:12
  286.2 13.5 %collective-permute-start.19 = (f32[384]{0:T(512)S(1)}, f32[384]{0:T(512)S(1)}, u32[]{:S(2)}, u32[]{:S(2)}) collective-permute-start(f32[384]{0:T(512)S(1)} %add_select_fusion.1), channel_id=1, source_target_pairs={{222,0},{223,1},{224,2},{225,3},{226,4},{227,5},{228,6},{229,7},{2... | collective-permute-start | bytes 4616 | tf_op jit(solution)/shard_map/ppermute | solution.py:12
  295.5 20.1 %collective-permute-start.22 = (f32[384]{0:T(512)S(1)}, f32[384]{0:T(512)S(1)}, u32[]{:S(2)}, u32[]{:S(2)}) collective-permute-start(f32[384]{0:T(512)S(1)} %add_select_fusion.1), channel_id=1, source_target_pairs={{205,0},{206,1},{207,2},{208,3},{209,4},{210,5},{211,6},{212,7},{2... | collective-permute-start | bytes 4616 | tf_op jit(solution)/shard_map/ppermute | solution.py:12
  299.8 17.4 %collective-permute-start.25 = (f32[384]{0:T(512)S(1)}, f32[384]{0:T(512)S(1)}, u32[]{:S(2)}, u32[]{:S(2)}) collective-permute-start(f32[384]{0:T(512)S(1)} %add_select_fusion.1), channel_id=1, source_target_pairs={{188,0},{189,1},{190,2},{191,3},{192,4},{193,5},{194,6},{195,7},{1... | collective-permute-start | bytes 4616 | tf_op jit(solution)/shard_map/ppermute | solution.py:12
  305.6 15.8 %collective-permute-start.17 = (f32[384]{0:T(512)S(1)}, f32[384]{0:T(512)S(1)}, u32[]{:S(2)}, u32[]{:S(2)}) collective-permute-start(f32[384]{0:T(512)S(1)} %get-tuple-element.41), channel_id=1, source_target_pairs={{239,0},{240,1},{241,2},{242,3},{243,4},{244,5},{245,6},{246,7},{2... | collective-permute-start | bytes 4616 | tf_op jit(solution)/shard_map/ppermute | solution.py:12
  314.1 188.7 %collective-permute-start.28 = (bf16[384,1024]{1,0:T(8,128)(2,1)S(1)}, bf16[384,1024]{1,0:T(8,128)(2,1)S(1)}, u32[]{:S(2)}, u32[]{:S(2)}) collective-permute-start(bf16[384,1024]{1,0:T(8,128)(2,1)S(1)} %multiply_convert_fusion.3), channel_id=1, source_target_pairs={{17,0},{18,1},{19,2},{20,3},{21,4},{22,5},{23,6},{24,7},{25,8},{26... | collective-permute-start | bytes 2359304 | tf_op jit(solution)/shard_map/ppermute | solution.py:12
  315.6 219.7 %collective-permute-start.29 = (bf16[384,1024]{1,0:T(8,128)(2,1)S(1)}, bf16[384,1024]{1,0:T(8,128)(2,1)S(1)}, u32[]{:S(2)}, u32[]{:S(2)}) collective-permute-start(bf16[384,1024]{1,0:T(8,128)(2,1)S(1)} %multiply_convert_fusion.2), channel_id=1, source_target_pairs={{34,0},{35,1},{36,2},{37,3},{38,4},{39,5},{40,6},{41,7},{42,8},{43... | collective-permute-start | bytes 2359304 | tf_op jit(solution)/shard_map/ppermute | solution.py:12
  317.2 218.1 %collective-permute-start.30 = (bf16[384,1024]{1,0:T(8,128)(2,1)S(1)}, bf16[384,1024]{1,0:T(8,128)(2,1)S(1)}, u32[]{:S(2)}, u32[]{:S(2)}) collective-permute-start(bf16[384,1024]{1,0:T(8,128)(2,1)S(1)} %multiply_convert_fusion.1), channel_id=1, source_target_pairs={{51,0},{52,1},{53,2},{54,3},{55,4},{56,5},{57,6},{58,7},{59,8},{60... | collective-permute-start | bytes 2359304 | tf_op jit(solution)/shard_map/ppermute | solution.py:12
  321.5 239.0 %collective-permute-start.31 = (bf16[384,1024]{1,0:T(8,128)(2,1)S(1)}, bf16[384,1024]{1,0:T(8,128)(2,1)S(1)}, u32[]{:S(2)}, u32[]{:S(2)}) collective-permute-start(bf16[384,1024]{1,0:T(8,128)(2,1)S(1)} %multiply_convert_fusion), channel_id=1, source_target_pairs={{68,0},{69,1},{70,2},{71,3},{72,4},{73,5},{74,6},{75,7},{76,8},{77... | collective-permute-start | bytes 2359304 | tf_op jit(solution)/shard_map/ppermute | solution.py:12
  322.3 250.4 %collective-permute-start.18 = (bf16[384,1024]{1,0:T(8,128)(2,1)S(1)}, bf16[384,1024]{1,0:T(8,128)(2,1)S(1)}, u32[]{:S(2)}, u32[]{:S(2)}) collective-permute-start(bf16[384,1024]{1,0:T(8,128)(2,1)S(1)} %multiply_convert_fusion.7), channel_id=1, source_target_pairs={{17,0},{18,1},{19,2},{20,3},{21,4},{22,5},{23,6},{24,7},{25,8},{26... | collective-permute-start | bytes 2359304 | tf_op jit(solution)/shard_map/ppermute | solution.py:12
  502.8 78.4 %collective-permute-start.21 = (bf16[384,1024]{1,0:T(8,128)(2,1)S(1)}, bf16[384,1024]{1,0:T(8,128)(2,1)S(1)}, u32[]{:S(2)}, u32[]{:S(2)}) collective-permute-start(bf16[384,1024]{1,0:T(8,128)(2,1)S(1)} %multiply_convert_fusion.6), channel_id=1, source_target_pairs={{34,0},{35,1},{36,2},{37,3},{38,4},{39,5},{40,6},{41,7},{42,8},{43... | collective-permute-start | bytes 2359304 | tf_op jit(solution)/shard_map/ppermute | solution.py:12
  535.3 45.9 %collective-permute-start.24 = (bf16[384,1024]{1,0:T(8,128)(2,1)S(1)}, bf16[384,1024]{1,0:T(8,128)(2,1)S(1)}, u32[]{:S(2)}, u32[]{:S(2)}) collective-permute-start(bf16[384,1024]{1,0:T(8,128)(2,1)S(1)} %multiply_convert_fusion.5), channel_id=1, source_target_pairs={{51,0},{52,1},{53,2},{54,3},{55,4},{56,5},{57,6},{58,7},{59,8},{60... | collective-permute-start | bytes 2359304 | tf_op jit(solution)/shard_map/ppermute | solution.py:12
  535.3 54.3 %collective-permute-start.27 = (bf16[384,1024]{1,0:T(8,128)(2,1)S(1)}, bf16[384,1024]{1,0:T(8,128)(2,1)S(1)}, u32[]{:S(2)}, u32[]{:S(2)}) collective-permute-start(bf16[384,1024]{1,0:T(8,128)(2,1)S(1)} %multiply_convert_fusion.4), channel_id=1, source_target_pairs={{68,0},{69,1},{70,2},{71,3},{72,4},{73,5},{74,6},{75,7},{76,8},{77... | collective-permute-start | bytes 2359304 | tf_op jit(solution)/shard_map/ppermute | solution.py:12
  (3 other events, 119.5 us)
where the time goes:
time: 601 us; the launch traced here: 592 us
  waiting for transfers between devices  374 us (62%)
  starting transfers between devices  190 us (32%)
  matrix products  23.4 us (4%)
    ppermute x32, waiting for transfers between devices, shifted(): return lax.ppermute(block, axis, route)  374 us
    ppermute x32, starting transfers between devices, shifted(): return lax.ppermute(block, axis, route)  190 us
  transfers between devices with their start and end apart: 32, of which 12 were waited for; matrix products, arithmetic and copies ran while one was open for 4% of the time, Pallas kernels for 0%

commit v1 on v0

v1 whole, which is shorter than its diff:
```python
import jax
import jax.numpy as jnp
from jax import lax
from jax.experimental import pallas as pl
from jax.experimental.pallas import tpu as pltpu
from jax.sharding import PartitionSpec as P

MESH = pl.DeviceIdType.MESH
LOGIT_SCALE = 20.0
N = 384
E = 1024
C = 3
R = N // C
STRIP = 32
ROW_OFFS = (1, -1, 2, -2)
COL_OFFS = (3, -3, 6, -6)


def kernel(q_ref, d_ref, p_ref, loss_ref, gq_ref, gd_ref,
           qc, dc, s, w, lcol, prow, pcol, rrow, rcol, mrow, mcol,
           outq, outd, inq, ind, accq, accd,
           loc_sem, lse_ssem, lse_rsem, f_ssem, f_rsem, b_ssem, b_rsem, o_sem):
    me = lax.axis_index("dx") * 16 + lax.axis_index("dy")

    def dev(o):
        k = lax.rem(me + (17 * o) % 256, 256)
        return (lax.div(k, 16), lax.rem(k, 16))

    def rcopy(src, dst, ss, rs, o):
        return pltpu.make_async_remote_copy(
            src_ref=src, dst_ref=dst, send_sem=ss, recv_sem=rs,
            device_id=dev(o), device_id_type=MESH)

    own_q = pltpu.make_async_copy(q_ref, qc.at[pl.ds(N, N)], loc_sem.at[0])
    own_d = pltpu.make_async_copy(d_ref, dc.at[pl.ds(N, N)], loc_sem.at[1])
    own_q.start()
    own_d.start()

    barrier = pltpu.get_barrier_semaphore()
    for o in ROW_OFFS + COL_OFFS:
        pl.semaphore_signal(barrier, inc=1, device_id=dev(o), device_id_type=MESH)
    pl.semaphore_wait(barrier, 8)
    own_q.wait()
    own_d.wait()

    def fwd(buf, kind, side, j, o):
        slot = 0 if side == 0 else 2
        return rcopy(buf.at[pl.ds(N + j * R, R)], buf.at[pl.ds(slot * N + j * R, R)],
                     f_ssem.at[kind, side, j], f_rsem.at[kind, side, j], o)

    sends = []
    for j in range(C):
        for kind, buf, o in ((0, qc, 1), (1, dc, 3)):
            for side in (0, 1):
                cp = fwd(buf, kind, side, j, o if side == 0 else -o)
                cp.start()
                sends.append(cp)

    def score(a, b, rows, r0):
        s[pl.ds(a * N + r0, rows), pl.ds(b * N, N)] = LOGIT_SCALE * lax.dot_general(
            qc[pl.ds(a * N + r0, rows), :], dc[pl.ds(b * N, N), :],
            (((1,), (1,)), ((), ())), preferred_element_type=jnp.float32)

    score(1, 1, N, 0)
    for j in range(C):
        for side in (1, 0):
            fwd(qc, 0, side, j, 1).wait_recv()
            score(0 if side == 0 else 2, 1, R, j * R)
    for side in (1, 0):
        for j in range(C):
            fwd(dc, 1, side, j, 3).wait_recv()
        b = 0 if side == 0 else 2

        @pl.loop(0, 3)
        def _(a):
            s[pl.ds(pl.multiple_of(a * N, N), N), pl.ds(b * N, N)] = LOGIT_SCALE * lax.dot_general(
                qc[pl.ds(pl.multiple_of(a * N, N), N), :], dc[pl.ds(b * N, N), :],
                (((1,), (1,)), ((), ())), preferred_element_type=jnp.float32)

    nstrip = 3 * N // STRIP
    W3 = 3 * N

    def row_pass(i, cmax):
        rows = pl.ds(pl.multiple_of(i * STRIP, STRIP), STRIP)
        x = s[rows, :]
        m = jnp.max(x, axis=1, keepdims=True)
        t = jnp.sum(jnp.exp(x - m), axis=1, keepdims=True)
        lcol[rows, :] = jnp.broadcast_to(m + jnp.log(t), (STRIP, 128))
        return jnp.maximum(cmax, jnp.max(x.reshape(STRIP // 8, 8, W3), axis=0))

    cmax = lax.fori_loop(0, nstrip, row_pass, jnp.full((8, W3), -jnp.inf, jnp.float32))
    cmax = jnp.max(cmax, axis=0, keepdims=True)

    def col_pass(i, acc):
        rows = pl.ds(pl.multiple_of(i * STRIP, STRIP), STRIP)
        e = jnp.exp(s[rows, :] - cmax)
        return acc + jnp.sum(e.reshape(STRIP // 8, 8, W3), axis=0)

    csum = lax.fori_loop(0, nstrip, col_pass, jnp.zeros((8, W3), jnp.float32))
    clse = cmax + jnp.log(jnp.sum(csum, axis=0, keepdims=True))
    for b in range(3):
        pcol[b:b + 1, :] = clse[:, b * N:(b + 1) * N]
        prow[b:b + 1, :] = lcol[b * N:(b + 1) * N, :].T[0:1, :]
    prow[3:8, :] = jnp.zeros((5, N), jnp.float32)
    pcol[3:8, :] = jnp.zeros((5, N), jnp.float32)

    lse_copies = []
    for g, (part, got, offs) in enumerate(((prow, rrow, ROW_OFFS), (pcol, rcol, COL_OFFS))):
        for i, o in enumerate(offs):
            cp = rcopy(part, got.at[i], lse_ssem.at[g, i], lse_rsem.at[g, i], -o)
            cp.start()
            lse_copies.append(cp)
    for cp in lse_copies:
        cp.wait_recv()

    def merge(part, got, out):
        def lae3(x, y, z):
            m = jnp.maximum(jnp.maximum(x, y), z)
            return m + jnp.log(jnp.exp(x - m) + jnp.exp(y - m) + jnp.exp(z - m))
        out[0:1, :] = lae3(part[0:1, :], got[1, 1:2, :], got[3, 2:3, :])
        out[1:2, :] = lae3(part[1:2, :], got[0, 0:1, :], got[1, 2:3, :])
        out[2:3, :] = lae3(part[2:3, :], got[0, 1:2, :], got[2, 0:1, :])

    merge(prow, rrow, mrow)
    merge(pcol, rcol, mcol)
    for a in range(3):
        lcol[a * N:(a + 1) * N, :] = jnp.broadcast_to(mrow[a:a + 1, :], (128, N)).T
    pos = lax.rem(p_ref[0:1, :], N).astype(jnp.float32)
    accq[:, 0:128] = jnp.broadcast_to(pos, (128, N)).T

    def weights(a):
        @pl.loop(0, N // STRIP)
        def _(i):
            r0 = pl.multiple_of(i * STRIP, STRIP)
            rows = pl.ds(a * N + r0, STRIP)
            rl = lcol[rows, 0:1]
            for b in range(3):
                x = s[rows, b * N:(b + 1) * N]
                v = 0.5 * (jnp.exp(x - rl) + jnp.exp(x - mcol[b:b + 1, :]))
                if a == 1 and b == 1:
                    local = accq[pl.ds(r0, STRIP), 0:1].astype(jnp.int32)
                    hit = lax.broadcasted_iota(jnp.int32, (STRIP, N), 1) == local
                    v = v - hit.astype(jnp.float32)
                    score_at = jnp.sum(jnp.where(hit, x, 0.0), axis=1, keepdims=True)
                    col_at = jnp.sum(jnp.where(hit, mcol[1:2, :], 0.0), axis=1, keepdims=True)
                    loss = 0.5 * (rl - score_at) + 0.5 * (col_at - score_at)
                    accd[pl.ds(r0, STRIP), 0:128] = jnp.broadcast_to(loss, (STRIP, 128))
                w[rows, b * N:(b + 1) * N] = v.astype(jnp.bfloat16)

    def row_product(a, out):
        @pl.loop(0, E // 256)
        def _(n):
            cols = pl.ds(pl.multiple_of(n * 256, 256), 256)
            out[:, cols] = jnp.dot(w[a * N:(a + 1) * N, :], dc[:, cols],
                                   preferred_element_type=jnp.float32).astype(out.dtype)

    def col_product(b, out):
        @pl.loop(0, E // 256)
        def _(n):
            cols = pl.ds(pl.multiple_of(n * 256, 256), 256)
            out[:, cols] = lax.dot_general(
                w[:, b * N:(b + 1) * N], qc[:, cols], (((0,), (0,)), ((), ())),
                preferred_element_type=jnp.float32).astype(out.dtype)

    def back(kind, side, j, o):
        buf, got = ((outq, inq), (outd, ind))[kind]
        return rcopy(buf.at[side, pl.ds(j * R, R)], got.at[side, pl.ds(j * R, R)],
                     b_ssem.at[kind, side, j], b_rsem.at[kind, side, j], o)

    def send_back(kind, side):
        o = (1, 3)[kind]
        for j in range(C):
            cp = back(kind, side, j, o if side == 1 else -o)
            cp.start()
            sends.append(cp)

    weights(2)
    row_product(2, outq.at[1])
    send_back(0, 1)
    weights(0)
    row_product(0, outq.at[0])
    send_back(0, 0)
    weights(1)
    loss_ref[0:1, :] = accd[:, 0:128].T[0:1, :]
    col_product(2, outd.at[1])
    send_back(1, 1)
    col_product(0, outd.at[0])
    send_back(1, 0)
    row_product(1, accq)
    col_product(1, accd)

    outs = []
    for kind, acc, got, res in ((0, accq, inq, gq_ref), (1, accd, ind, gd_ref)):
        for j in range(C):
            for side in (0, 1):
                back(kind, side, j, 1).wait_recv()
            rows = pl.ds(j * R, R)
            acc[rows, :] = LOGIT_SCALE * (
                acc[rows, :] + got[0, rows, :].astype(jnp.float32) + got[1, rows, :].astype(jnp.float32))
            cp = pltpu.make_async_copy(acc.at[rows], res.at[rows], o_sem.at[kind, j])
            cp.start()
            outs.append(cp)
    for cp in sends + lse_copies:
        cp.wait_send()
    for cp in outs:
        cp.wait()


def per_device(queries, documents, positives):
    f32, bf16 = jnp.float32, jnp.bfloat16
    dma = pltpu.SemaphoreType.DMA
    loss, gq, gd = pl.pallas_call(
        kernel,
        out_shape=(jax.ShapeDtypeStruct((1, N), f32),
                   jax.ShapeDtypeStruct((N, E), f32),
                   jax.ShapeDtypeStruct((N, E), f32)),
        in_specs=[pl.BlockSpec(memory_space=pl.ANY), pl.BlockSpec(memory_space=pl.ANY),
                  pl.BlockSpec(memory_space=pltpu.VMEM)],
        out_specs=(pl.BlockSpec(memory_space=pltpu.VMEM), pl.BlockSpec(memory_space=pl.ANY),
                   pl.BlockSpec(memory_space=pl.ANY)),
        scratch_shapes=[
            pltpu.VMEM((3 * N, E), bf16), pltpu.VMEM((3 * N, E), bf16),
            pltpu.VMEM((3 * N, 3 * N), f32), pltpu.VMEM((3 * N, 3 * N), bf16),
            pltpu.VMEM((3 * N, 128), f32),
            pltpu.VMEM((8, N), f32), pltpu.VMEM((8, N), f32),
            pltpu.VMEM((4, 8, N), f32), pltpu.VMEM((4, 8, N), f32),
            pltpu.VMEM((8, N), f32), pltpu.VMEM((8, N), f32),
            pltpu.VMEM((2, N, E), bf16), pltpu.VMEM((2, N, E), bf16),
            pltpu.VMEM((2, N, E), bf16), pltpu.VMEM((2, N, E), bf16),
            pltpu.VMEM((N, E), f32), pltpu.VMEM((N, E), f32),
            dma((2,)), dma((2, 4)), dma((2, 4)),
            dma((2, 2, C)), dma((2, 2, C)), dma((2, 2, C)), dma((2, 2, C)), dma((2, C)),
        ],
        compiler_params=pltpu.CompilerParams(
            collective_id=0, has_side_effects=True, vmem_limit_bytes=48 * 1024 * 1024),
        cost_estimate=pl.CostEstimate(flops=8_200_000_000, bytes_accessed=8_000_000,
                                      transcendentals=5_400_000),
    )(queries, documents, positives.reshape(1, N))
    return loss.reshape(N), gq, gd


def solution(mesh):
    return jax.shard_map(
        per_device,
        mesh=mesh,
        in_specs=(P(("dx", "dy"), None), P(("dx", "dy"), None), P(("dx", "dy"))),
        out_specs=(P(("dx", "dy")), P(("dx", "dy"), None), P(("dx", "dy"), None)),
        check_vma=False,
    )
```

time: 601 us -> 232 us (0.39)
  the two profiles are of different devices: /device:TPU:6 before, /device:TPU:1 now
where the time goes in v1:
time: 232 us; the launch traced here: 229 us
  Pallas kernels  223 us (96%)
  local copies, waits for them, and re-layouts  5.23 us (2%)
    pallas_call x1, Pallas kernels, per_device(): pl.pallas_call(kernel, out_shape=(jax.ShapeDtypeStruct((1, N), f32), jax....  223 us

profile of v1, /device:TPU:1, one launch (start us, length us, event | category | flops | bytes accessed | tf_op | source)
XLA Modules:
  0.0 229.1 jit_solution(4542008582137737929)
XLA Ops:
  0.6 0.7 reshape.12.p_ref
  1.3 0.0 copy-start
  1.3 1.1 copy-done
  2.4 0.0 copy-start.1
  2.5 1.1 copy-done.1
  3.6 222.6 %shard_map.58 = (f32[1,384]{1,0:T(1,128)S(1)}, f32[384,1024]{1,0:T(8,128)S(1)}, f32[384,1024]{1,0:T(8,128)S(1)}) custom-call(bf16[384,1024]{1,0:T(8,128)(2,1)S(1)} %copy-done, bf16[384,1024]{1,0:T(8,128)(2,1)S(1)} %copy-done.1, s32[1,384]{1,0:T(1,128)S(1)} %reshape.12.p_ref), custom_call_target="tpu_custom_call" | custom-call | flops 8200000000 | bytes 8000000 | tf_op jit(solution)/shard_map/pallas_call | solution.py:212
  226.2 0.6 reduce
  226.8 1.1 copy.8
  227.9 1.1 copy.9
Async XLA Ops:
  1.3 1.1 copy-start
  2.4 1.1 copy-start.1

commit v2 on v0

v2 whole, which is shorter than its diff:
```python
import jax
import jax.numpy as jnp
from jax import lax
from jax.experimental import pallas as pl
from jax.experimental.pallas import tpu as pltpu
from jax.sharding import PartitionSpec as P

MESH = pl.DeviceIdType.MESH
LOGIT_SCALE = 20.0
N = 384
E = 1024
W3 = 3 * N
C = 6
R = N // C
STRIP = 32
OFFS = (1, 3)
FWD_MODES = ((384, 128, 41060, 24673, 38937, 38938, 34340, 1537), (43590, 43622, 10377, 43173, 34852, 35345, 34197, 35092))
BACK_MODES = ((384, 384, 8292, 8801, 18457, 38937, 34368, 1537), (27221, 34918, 10385, 10373, 34065, 35353, 42261, 35348))


def spot(q, plus):
    return (q // 2) * 4 * R + plus * 2 * R + (q % 2) * R


def kernel(q_ref, d_ref, p_ref, loss_ref, gq_ref, gd_ref,
           qc, dc, s, w, lcol, part, got, full, outb, inb, rel, acc,
           loc_sem, lse_ssem, lse_rsem, f_ssem, f_rsem, g_ssem, b_ssem, b_rsem, r_ssem, r_rsem, o_sem):
    me = lax.axis_index("dx") * 16 + lax.axis_index("dy")
    ring = lax.rem(me * 241, 256)
    cat = (qc, dc)
    src = (q_ref, d_ref)

    def dev(o):
        k = lax.rem(me + (17 * o) % 256, 256)
        return (lax.div(k, 16), lax.rem(k, 16))

    def mode_of(words, o):
        t = lax.rem(ring + (o % 64), 64)
        hi, lo = lax.div(t, 8), lax.rem(t, 8)
        word = jnp.int32(0)
        for i, v in enumerate(words):
            word = jnp.where(hi == i, jnp.int32(v), word)
        out = jnp.int32(0)
        for i in range(8):
            out = jnp.where(lo == i, lax.rem(lax.div(word, jnp.int32(4 ** i)), 4), out)
        return out

    def rcopy(a, b, ss, rs, o):
        return pltpu.make_async_remote_copy(
            src_ref=a, dst_ref=b, send_sem=ss, recv_sem=rs,
            device_id=dev(o), device_id_type=MESH)

    own = [pltpu.make_async_copy(src[k], cat[k].at[pl.ds(0, N)], loc_sem.at[k]) for k in (0, 1)]
    for cp in own:
        cp.start()

    barrier = pltpu.get_barrier_semaphore()
    for o in (1, -1, 2, -2, 3, -3, 6, -6):
        pl.semaphore_signal(barrier, inc=1, device_id=dev(o), device_id_type=MESH)
    fmode = [[mode_of(FWD_MODES[k], d * OFFS[k]) for d in (-1, 1, 0)] for k in (0, 1)]
    bmode = [[mode_of(BACK_MODES[k], d * OFFS[k]) for d in (-1, 1, 0)] for k in (0, 1)]
    pl.semaphore_wait(barrier, 8)

    def slot(k, plus, q):
        return cat[k].at[pl.ds(N + spot(q, plus), R)]

    def send(k, plus, q):
        o = OFFS[k] if plus == 0 else -OFFS[k]
        return rcopy(src[k].at[pl.ds(q * R, R)], slot(k, plus, q),
                     f_ssem.at[k, plus, q], f_rsem.at[k, plus, q], o)

    def forward(k, plus, q):
        o = -2 * OFFS[k] if plus == 0 else 2 * OFFS[k]
        return rcopy(slot(k, plus, q), slot(k, 1 - plus, q),
                     g_ssem.at[k, plus, q], f_rsem.at[k, 1 - plus, q], o)

    def relays(k, plus):
        return fmode[k][plus] == (1 if plus == 0 else 2)

    def sends_to(k, plus):
        return fmode[k][2] != (2 if plus == 0 else 1)

    for q in range(C):
        for k in (0, 1):
            for plus in (0, 1):
                @pl.when(sends_to(k, plus))
                def _():
                    send(k, plus, q).start()

    def pass_on(q):
        for k in (0, 1):
            for plus in (0, 1):
                @pl.when(relays(k, plus))
                def _():
                    send(k, plus, q).wait_recv()
                    forward(k, plus, q).start()

    def take(q):
        for k in (0, 1):
            for plus in (0, 1):
                @pl.when(jnp.logical_not(relays(k, plus)))
                def _():
                    send(k, plus, q).wait_recv()

    for cp in own:
        cp.wait()

    def score(g, r0, r1, c0, c1):
        s[g, r0:r1, c0:c1] = LOGIT_SCALE * lax.dot_general(
            cat[g][r0:r1, :], cat[1 - g][c0:c1, :],
            (((1,), (1,)), ((), ())), preferred_element_type=jnp.float32)

    def log_sum(g, r0, r1, c0, c1):
        n = c1 - c0
        steps = (r1 - r0) // STRIP

        def strip(i):
            return s[g, pl.ds(pl.multiple_of(r0 + i * STRIP, STRIP), STRIP), c0:c1]

        def top(i, m):
            return jnp.maximum(m, jnp.max(strip(i).reshape(STRIP // 8, 8, n), axis=0))

        m = lax.fori_loop(0, steps, top, jnp.full((8, n), -jnp.inf, jnp.float32))
        m = jnp.max(m, axis=0, keepdims=True)

        def add(i, t):
            return t + jnp.sum(jnp.exp(strip(i) - m).reshape(STRIP // 8, 8, n), axis=0)

        t = lax.fori_loop(0, steps, add, jnp.zeros((8, n), jnp.float32))
        return m + jnp.log(jnp.sum(t, axis=0, keepdims=True))

    def scores_step(j):
        base = N + j * 4 * R if j >= 0 else 0
        end = base + 4 * R if j >= 0 else N
        for g in (0, 1):
            score(g, base, end, 0, end)
            if j >= 0:
                score(g, 0, base, base, end)
        for g in (0, 1):
            if j >= 0:
                x = part[g, :, 0:base]
                y = log_sum(g, base, end, 0, base)
                m = jnp.maximum(x, y)
                part[g, :, 0:base] = m + jnp.log(jnp.exp(x - m) + jnp.exp(y - m))
            part[g, :, base:end] = log_sum(g, 0, end, base, end)

    scores_step(-1)
    for q in range(3):
        pass_on(q)
    take(0)
    take(1)
    scores_step(0)
    pass_on(3)
    pass_on(4)
    take(2)
    take(3)
    scores_step(1)
    pass_on(5)
    take(4)
    take(5)
    scores_step(2)

    lse_copies = []
    for g in (0, 1):
        for i, d in enumerate((1, -1, 2, -2)):
            cp = rcopy(part.at[g], got.at[g, i], lse_ssem.at[g, i], lse_rsem.at[g, i], -d * OFFS[1 - g])
            cp.start()
            lse_copies.append(cp)
    for cp in lse_copies:
        cp.wait_recv()

    def lae3(x, y, z):
        m = jnp.maximum(jnp.maximum(x, y), z)
        return m + jnp.log(jnp.exp(x - m) + jnp.exp(y - m) + jnp.exp(z - m))

    for g in (0, 1):
        for j in range(3):
            o, b, a = 128 * j, N + 256 * j, N + 256 * j + 128
            mine, up, down, up2, down2 = part.at[g], got.at[g, 0], got.at[g, 1], got.at[g, 2], got.at[g, 3]
            full[g, :, o:o + 128] = lae3(mine[:, o:o + 128], up[:, b:b + 128], down[:, a:a + 128])
            full[g, :, a:a + 128] = lae3(mine[:, a:a + 128], up[:, o:o + 128], up2[:, b:b + 128])
            full[g, :, b:b + 128] = lae3(mine[:, b:b + 128], down[:, o:o + 128], down2[:, a:a + 128])
    for g in (0, 1):
        for i in range(9):
            lcol[g, i * 128:(i + 1) * 128, :] = jnp.broadcast_to(
                full[1 - g, :, i * 128:(i + 1) * 128], (128, 128)).T

    def weigh(g, rows):
        x = s[g, rows, :]
        return x, 0.5 * (jnp.exp(x - lcol[g, rows, 0:1]) + jnp.exp(x - full[g]))

    def weights(g, r0, r1):
        @pl.loop(0, (r1 - r0) // STRIP)
        def _(i):
            rows = pl.ds(pl.multiple_of(r0 + i * STRIP, STRIP), STRIP)
            w[g, rows, :] = weigh(g, rows)[1].astype(jnp.bfloat16)

    def product(g, r0, rows, out, o0):
        @pl.loop(0, E // 256)
        def _(n):
            cols = pl.ds(pl.multiple_of(n * 256, 256), 256)
            out[o0:o0 + rows, cols] = jnp.dot(
                w[g, r0:r0 + rows, :], cat[1 - g][:, cols],
                preferred_element_type=jnp.float32).astype(out.dtype)

    def give(k, plus, q):
        o = OFFS[k] if plus == 1 else -OFFS[k]
        return rcopy(outb.at[k, pl.ds(spot(q, plus), R)], inb.at[k, pl.ds(spot(q, 1 - plus), R)],
                     b_ssem.at[k, plus, q], b_rsem.at[k, 1 - plus, q], o)

    def lend(k, plus, q):
        o = 2 * OFFS[k] if plus == 1 else -2 * OFFS[k]
        return rcopy(outb.at[k, pl.ds(spot(q, plus), R)], rel.at[k, pl.ds(spot(q, 1 - plus), R)],
                     r_ssem.at[k, plus, q], r_rsem.at[k, 1 - plus, q], o)

    def is_star(k, plus):
        return bmode[k][plus] == 0

    def is_leaf(k, plus):
        return bmode[k][plus] == (1 if plus == 1 else 2)

    def is_relay(k, plus):
        return bmode[k][plus] == (2 if plus == 1 else 1)

    for k in (0, 1):
        for j in range(3):
            weights(k, N + 256 * j, N + 256 * j + 256)
            product(k, N + 256 * j, 256, outb.at[k], 256 * j)
            for q in (2 * j, 2 * j + 1):
                for plus in (0, 1):
                    @pl.when(is_leaf(k, plus))
                    def _():
                        lend(k, plus, q).start()

                    @pl.when(is_star(k, plus))
                    def _():
                        give(k, plus, q).start()

    def relay_back(k, q):
        for plus in (0, 1):
            @pl.when(is_relay(k, plus))
            def _():
                lend(k, 1 - plus, q).wait_recv()
                rows = pl.ds(spot(q, plus), R)
                outb[k, rows, :] = (outb[k, rows, :].astype(jnp.float32)
                                    + rel[k, rows, :].astype(jnp.float32)).astype(jnp.bfloat16)
                give(k, plus, q).start()

    for q in range(C):
        relay_back(0, q)

    weights(1, 0, N)
    weights(0, 0, N)
    pos = lax.rem(p_ref[...], N)
    acc[0, 0:N, 0:128] = jnp.broadcast_to(pos.astype(jnp.float32), (128, N)).T
    hit = lax.broadcasted_iota(jnp.int32, (N, N), 0) == pos
    x = s[1, 0:N, 0:N]
    score_at = jnp.sum(jnp.where(hit, x, 0.0), axis=0, keepdims=True)
    col_at = jnp.sum(jnp.where(hit, lcol[1, 0:N, 0:1], 0.0), axis=0, keepdims=True)
    loss_ref[...] = 0.5 * (full[1, :, 0:N] - score_at) + 0.5 * (col_at - score_at)

    @pl.loop(0, N // STRIP)
    def _(i):
        rows = pl.ds(pl.multiple_of(i * STRIP, STRIP), STRIP)
        iota0 = lax.broadcasted_iota(jnp.int32, (STRIP, N), 0) + i * STRIP
        iota1 = lax.broadcasted_iota(jnp.int32, (STRIP, N), 1)
        at = acc[0, rows, 0:1].astype(jnp.int32)
        for g, match in ((0, iota1 == at), (1, iota0 == pos)):
            x = s[g, rows, 0:N]
            v = 0.5 * (jnp.exp(x - lcol[g, rows, 0:1]) + jnp.exp(x - full[g, :, 0:N]))
            w[g, rows, 0:N] = (v - match.astype(jnp.float32)).astype(jnp.bfloat16)

    for q in range(C):
        relay_back(1, q)
    product(0, 0, N, acc.at[0], 0)
    product(1, 0, N, acc.at[1], 0)

    outs = []
    for k, res in ((0, gq_ref), (1, gd_ref)):
        for q in range(C):
            rows = pl.ds(q * R, R)
            lo, hi = pl.ds(spot(q, 0), R), pl.ds(spot(q, 1), R)

            @pl.when(bmode[k][2] != 1)
            def _():
                give(k, 1, q).wait_recv()
                acc[k, rows, :] = acc[k, rows, :] + inb[k, lo, :].astype(jnp.float32)

            @pl.when(bmode[k][2] != 2)
            def _():
                give(k, 0, q).wait_recv()
                acc[k, rows, :] = acc[k, rows, :] + inb[k, hi, :].astype(jnp.float32)

            acc[k, rows, :] = LOGIT_SCALE * acc[k, rows, :]
            cp = pltpu.make_async_copy(acc.at[k, rows], res.at[rows], o_sem.at[k, q])
            cp.start()
            outs.append(cp)

    for k in (0, 1):
        for q in range(C):
            for plus in (0, 1):
                @pl.when(sends_to(k, plus))
                def _():
                    send(k, plus, q).wait_send()

                @pl.when(relays(k, plus))
                def _():
                    forward(k, plus, q).wait_send()

                @pl.when(is_leaf(k, plus))
                def _():
                    lend(k, plus, q).wait_send()

                @pl.when(jnp.logical_not(is_leaf(k, plus)))
                def _():
                    give(k, plus, q).wait_send()
    for cp in lse_copies:
        cp.wait_send()
    for cp in outs:
        cp.wait()


def per_device(queries, documents, positives):
    f32, bf16 = jnp.float32, jnp.bfloat16
    dma = pltpu.SemaphoreType.DMA
    loss, gq, gd = pl.pallas_call(
        kernel,
        out_shape=(jax.ShapeDtypeStruct((1, N), f32),
                   jax.ShapeDtypeStruct((N, E), f32),
                   jax.ShapeDtypeStruct((N, E), f32)),
        in_specs=[pl.BlockSpec(memory_space=pl.ANY), pl.BlockSpec(memory_space=pl.ANY),
                  pl.BlockSpec(memory_space=pltpu.VMEM)],
        out_specs=(pl.BlockSpec(memory_space=pltpu.VMEM), pl.BlockSpec(memory_space=pl.ANY),
                   pl.BlockSpec(memory_space=pl.ANY)),
        scratch_shapes=[
            pltpu.VMEM((W3, E), bf16), pltpu.VMEM((W3, E), bf16),
            pltpu.VMEM((2, W3, W3), f32), pltpu.VMEM((2, W3, W3), bf16),
            pltpu.VMEM((2, W3, 128), f32),
            pltpu.VMEM((2, 1, W3), f32), pltpu.VMEM((2, 4, 1, W3), f32), pltpu.VMEM((2, 1, W3), f32),
            pltpu.VMEM((2, 2 * N, E), bf16), pltpu.VMEM((2, 2 * N, E), bf16), pltpu.VMEM((2, 2 * N, E), bf16),
            pltpu.VMEM((2, N, E), f32),
            dma((2,)), dma((2, 4)), dma((2, 4)),
            dma((2, 2, C)), dma((2, 2, C)), dma((2, 2, C)), dma((2, 2, C)), dma((2, 2, C)),
            dma((2, 2, C)), dma((2, 2, C)), dma((2, C)),
        ],
        compiler_params=pltpu.CompilerParams(
            collective_id=0, has_side_effects=True, vmem_limit_bytes=60 * 1024 * 1024),
        cost_estimate=pl.CostEstimate(flops=11_000_000_000, bytes_accessed=8_000_000,
                                      transcendentals=11_000_000),
    )(queries, documents, positives.reshape(1, N))
    return loss.reshape(N), gq, gd


def solution(mesh):
    return jax.shard_map(
        per_device,
        mesh=mesh,
        in_specs=(P(("dx", "dy"), None), P(("dx", "dy"), None), P(("dx", "dy"))),
        out_specs=(P(("dx", "dy")), P(("dx", "dy"), None), P(("dx", "dy"), None)),
        check_vma=False,
    )
```

time: 601 us -> 194 us (0.32)
  the two profiles are of different devices: /device:TPU:6 before, /device:TPU:58 now
where the time goes in v2:
time: 194 us
  Pallas kernels  186 us (96%)
  local copies, waits for them, and re-layouts  5.24 us (3%)
    pallas_call x1, Pallas kernels, per_device(): pl.pallas_call(kernel, out_shape=(jax.ShapeDtypeStruct((1, N), f32), jax....  186 us
    unnamed x4, local copies, waits for them, and re-layouts  3.99 us

profile of v2, /device:TPU:58, one launch (start us, length us, event | category | flops | bytes accessed | tf_op | source)
XLA Modules:
  0.0 193.6 jit_solution(4809039441069695103)
XLA Ops:
  0.6 1.2 reshape.12.p_ref
  1.9 186.5 %shard_map.58 = (f32[1,384]{1,0:T(1,128)}, f32[384,1024]{1,0:T(8,128)}, f32[384,1024]{1,0:T(8,128)}) custom-call(bf16[384,1024]{1,0:T(8,128)(2,1)} %q_ref.1, bf16[384,1024]{1,0:T(8,128)(2,1)} %d_ref.1, s32[1,384]{1,0:T(1,128)} %reshape.12.p_ref), custom_call_target="tpu_custom_call" | custom-call | flops 11000000512 | bytes 8000000 | tf_op jit(solution)/shard_map/pallas_call | solution.py:326
  188.4 1.3 reduce
  189.6 0.0 copy-start
  189.6 2.8 %copy.8 = f32[384,1024]{1,0:T(8,128)} copy(f32[384,1024]{1,0:T(8,128)} %get-tuple-element.13) | data formatting | bytes 3145728
  192.5 0.0 copy-done
  192.5 1.1 copy.9
Async XLA Ops:
  189.6 2.9 %copy-start = (f32[384,1024]{1,0:T(8,128)S(1)}, f32[384,1024]{1,0:T(8,128)}, u32[]{:S(2)}) copy-start(f32[384,1024]{1,0:T(8,128)} %get-tuple-element.14) | copy-start | bytes 4718596

commit v3 on v2

--- a/solution.py
+++ b/solution.py
@@ -13,22 +13,24 @@
 C = 6
 R = N // C
 STRIP = 32
+ORDER = ((1, 0), (1, 1), (0, 0), (0, 1), (1, 2), (1, 3), (0, 2), (0, 3), (1, 4), (1, 5), (0, 4), (0, 5))
 OFFS = (1, 3)
-FWD_MODES = ((384, 128, 41060, 24673, 38937, 38938, 34340, 1537), (43590, 43622, 10377, 43173, 34852, 35345, 34197, 35092))
-BACK_MODES = ((384, 384, 8292, 8801, 18457, 38937, 34368, 1537), (27221, 34918, 10385, 10373, 34065, 35353, 42261, 35348))
+FWD_MODES = ((8584, 130, 70, 33, 38937, 38937, 33792, 514), (27206, 41494, 10256, 10400, 34833, 10256, 33045, 32788))
+BACK_MODES = ((16512, 0, 512, 96, 34840, 4113, 1024, 4), (32833, 43521, 2180, 8577, 2321, 2194, 42244, 16))
 
 
 def spot(q, plus):
     return (q // 2) * 4 * R + plus * 2 * R + (q % 2) * R
 
 
-def kernel(q_ref, d_ref, p_ref, loss_ref, gq_ref, gd_ref,
-           qc, dc, s, w, lcol, part, got, full, outb, inb, rel, acc,
-           loc_sem, lse_ssem, lse_rsem, f_ssem, f_rsem, g_ssem, b_ssem, b_rsem, r_ssem, r_rsem, o_sem):
+def kernel(q_ref, d_ref, p_ref, loss_ref, accq_ref, accd_ref, inq_ref, ind_ref,
+           qc, dc, s, w, lcol, part, got, full, outb, rel, acc,
+           loc_sem, lse_ssem, lse_rsem, f_ssem, f_rsem, g_ssem, b_ssem, b_rsem, r_ssem, r_rsem, o_sem, z_sem):
     me = lax.axis_index("dx") * 16 + lax.axis_index("dy")
     ring = lax.rem(me * 241, 256)
     cat = (qc, dc)
     src = (q_ref, d_ref)
+    inb = (inq_ref, ind_ref)
 
     def dev(o):
         k = lax.rem(me + (17 * o) % 256, 256)
@@ -80,27 +82,24 @@
     def sends_to(k, plus):
         return fmode[k][2] != (2 if plus == 0 else 1)
 
-    for q in range(C):
-        for k in (0, 1):
-            for plus in (0, 1):
-                @pl.when(sends_to(k, plus))
-                def _():
-                    send(k, plus, q).start()
-
-    def pass_on(q):
-        for k in (0, 1):
-            for plus in (0, 1):
-                @pl.when(relays(k, plus))
-                def _():
-                    send(k, plus, q).wait_recv()
-                    forward(k, plus, q).start()
-
-    def take(q):
-        for k in (0, 1):
-            for plus in (0, 1):
-                @pl.when(jnp.logical_not(relays(k, plus)))
-                def _():
-                    send(k, plus, q).wait_recv()
+    for k, q in ORDER:
+        for plus in (0, 1):
+            @pl.when(sends_to(k, plus))
+            def _():
+                send(k, plus, q).start()
+
+    def pass_on(k, q):
+        for plus in (0, 1):
+            @pl.when(relays(k, plus))
+            def _():
+                send(k, plus, q).wait_recv()
+                forward(k, plus, q).start()
+
+    def take(k, q):
+        for plus in (0, 1):
+            @pl.when(jnp.logical_not(relays(k, plus)))
+            def _():
+                send(k, plus, q).wait_recv()
 
     for cp in own:
         cp.wait()
@@ -129,36 +128,39 @@
         t = lax.fori_loop(0, steps, add, jnp.zeros((8, n), jnp.float32))
         return m + jnp.log(jnp.sum(t, axis=0, keepdims=True))
 
-    def scores_step(j):
-        base = N + j * 4 * R if j >= 0 else 0
-        end = base + 4 * R if j >= 0 else N
-        for g in (0, 1):
-            score(g, base, end, 0, end)
-            if j >= 0:
-                score(g, 0, base, base, end)
-        for g in (0, 1):
-            if j >= 0:
-                x = part[g, :, 0:base]
-                y = log_sum(g, base, end, 0, base)
-                m = jnp.maximum(x, y)
-                part[g, :, 0:base] = m + jnp.log(jnp.exp(x - m) + jnp.exp(y - m))
-            part[g, :, base:end] = log_sum(g, 0, end, base, end)
-
-    scores_step(-1)
-    for q in range(3):
-        pass_on(q)
-    take(0)
-    take(1)
-    scores_step(0)
-    pass_on(3)
-    pass_on(4)
-    take(2)
-    take(3)
-    scores_step(1)
-    pass_on(5)
-    take(4)
-    take(5)
-    scores_step(2)
+    def append(k, r0, r1, n):
+        g = k
+        score(g, r0, r1, 0, n)
+        score(1 - g, 0, n, r0, r1)
+        y = log_sum(g, r0, r1, 0, n)
+        if r0 > 0:
+            x = part[g, :, 0:n]
+            m = jnp.maximum(x, y)
+            y = m + jnp.log(jnp.exp(x - m) + jnp.exp(y - m))
+        part[g, :, 0:n] = y
+        part[1 - g, :, r0:r1] = log_sum(1 - g, 0, n, r0, r1)
+
+    outb[0, 0:N, :] = jnp.zeros((N, E), jnp.bfloat16)
+
+    def zero_side(k, plus):
+        return pltpu.make_async_copy(outb.at[0, pl.ds(0, N)], inb[k].at[plus], z_sem.at[k, plus])
+
+    for k in (0, 1):
+        for plus in (0, 1):
+            @pl.when(bmode[k][2] == 1 + plus)
+            def _():
+                zero_side(k, plus).start()
+
+    append(0, 0, N, N)
+    plan = sorted([(i, 0, k, q) for i, (k, q) in enumerate(ORDER)] + [(i + 3, 1, k, q) for i, (k, q) in enumerate(ORDER)])
+    for _, late, k, q in plan:
+        if not late:
+            pass_on(k, q)
+        else:
+            take(k, q)
+            if q % 2 == 1:
+                base = N + (q // 2) * 4 * R
+                append(k, base, base + 4 * R, base + (4 * R if k == 0 else 0))
 
     lse_copies = []
     for g in (0, 1):
@@ -180,16 +182,17 @@
             full[g, :, o:o + 128] = lae3(mine[:, o:o + 128], up[:, b:b + 128], down[:, a:a + 128])
             full[g, :, a:a + 128] = lae3(mine[:, a:a + 128], up[:, o:o + 128], up2[:, b:b + 128])
             full[g, :, b:b + 128] = lae3(mine[:, b:b + 128], down[:, o:o + 128], down2[:, a:a + 128])
-    for g in (0, 1):
-        for i in range(9):
-            lcol[g, i * 128:(i + 1) * 128, :] = jnp.broadcast_to(
-                full[1 - g, :, i * 128:(i + 1) * 128], (128, 128)).T
+    def columns(g, r0, r1):
+        for r in range(r0, r1, 128):
+            lcol[g, r:r + 128, :] = jnp.broadcast_to(full[1 - g, :, r:r + 128], (128, 128)).T
 
     def weigh(g, rows):
         x = s[g, rows, :]
         return x, 0.5 * (jnp.exp(x - lcol[g, rows, 0:1]) + jnp.exp(x - full[g]))
 
     def weights(g, r0, r1):
+        columns(g, r0, r1)
+
         @pl.loop(0, (r1 - r0) // STRIP)
         def _(i):
             rows = pl.ds(pl.multiple_of(r0 + i * STRIP, STRIP), STRIP)
@@ -205,7 +208,7 @@
 
     def give(k, plus, q):
         o = OFFS[k] if plus == 1 else -OFFS[k]
-        return rcopy(outb.at[k, pl.ds(spot(q, plus), R)], inb.at[k, pl.ds(spot(q, 1 - plus), R)],
+        return rcopy(outb.at[k, pl.ds(spot(q, plus), R)], inb[k].at[1 - plus, pl.ds(q * R, R)],
                      b_ssem.at[k, plus, q], b_rsem.at[k, 1 - plus, q], o)
 
     def lend(k, plus, q):
@@ -223,6 +226,12 @@
         return bmode[k][plus] == (2 if plus == 1 else 1)
 
     for k in (0, 1):
+        for plus in (0, 1):
+            @pl.when(bmode[k][2] == 1 + plus)
+            def _():
+                zero_side(k, plus).wait()
+
+    for k in (1, 0):
         for j in range(3):
             weights(k, N + 256 * j, N + 256 * j + 256)
             product(k, N + 256 * j, 256, outb.at[k], 256 * j)
@@ -246,18 +255,17 @@
                                     + rel[k, rows, :].astype(jnp.float32)).astype(jnp.bfloat16)
                 give(k, plus, q).start()
 
-    for q in range(C):
-        relay_back(0, q)
-
+    relay_back(1, 0)
     weights(1, 0, N)
     weights(0, 0, N)
-    pos = lax.rem(p_ref[...], N)
+    pos = lax.rem(p_ref[...].reshape(1, N), N)
     acc[0, 0:N, 0:128] = jnp.broadcast_to(pos.astype(jnp.float32), (128, N)).T
     hit = lax.broadcasted_iota(jnp.int32, (N, N), 0) == pos
     x = s[1, 0:N, 0:N]
     score_at = jnp.sum(jnp.where(hit, x, 0.0), axis=0, keepdims=True)
     col_at = jnp.sum(jnp.where(hit, lcol[1, 0:N, 0:1], 0.0), axis=0, keepdims=True)
-    loss_ref[...] = 0.5 * (full[1, :, 0:N] - score_at) + 0.5 * (col_at - score_at)
+    loss_ref[...] = (0.5 * (full[1, :, 0:N] - score_at) + 0.5 * (col_at - score_at)).reshape(loss_ref.shape)
+    relay_back(1, 1)
 
     @pl.loop(0, N // STRIP)
     def _(i):
@@ -270,31 +278,27 @@
             v = 0.5 * (jnp.exp(x - lcol[g, rows, 0:1]) + jnp.exp(x - full[g, :, 0:N]))
             w[g, rows, 0:N] = (v - match.astype(jnp.float32)).astype(jnp.bfloat16)
 
+    relay_back(1, 2)
+    product(0, 0, N, acc.at[0], 0)
+    relay_back(1, 3)
+    product(1, 0, N, acc.at[1], 0)
+    relay_back(1, 4)
+    relay_back(1, 5)
     for q in range(C):
-        relay_back(1, q)
-    product(0, 0, N, acc.at[0], 0)
-    product(1, 0, N, acc.at[1], 0)
-
-    outs = []
-    for k, res in ((0, gq_ref), (1, gd_ref)):
+        relay_back(0, q)
+
+    outs = [pltpu.make_async_copy(acc.at[k], (accq_ref, accd_ref)[k], o_sem.at[k]) for k in (0, 1)]
+    for cp in outs:
+        cp.start()
+    for k in (1, 0):
         for q in range(C):
-            rows = pl.ds(q * R, R)
-            lo, hi = pl.ds(spot(q, 0), R), pl.ds(spot(q, 1), R)
-
             @pl.when(bmode[k][2] != 1)
             def _():
                 give(k, 1, q).wait_recv()
-                acc[k, rows, :] = acc[k, rows, :] + inb[k, lo, :].astype(jnp.float32)
 
             @pl.when(bmode[k][2] != 2)
             def _():
                 give(k, 0, q).wait_recv()
-                acc[k, rows, :] = acc[k, rows, :] + inb[k, hi, :].astype(jnp.float32)
-
-            acc[k, rows, :] = LOGIT_SCALE * acc[k, rows, :]
-            cp = pltpu.make_async_copy(acc.at[k, rows], res.at[rows], o_sem.at[k, q])
-            cp.start()
-            outs.append(cp)
 
     for k in (0, 1):
         for q in range(C):
@@ -323,32 +327,37 @@
 def per_device(queries, documents, positives):
     f32, bf16 = jnp.float32, jnp.bfloat16
     dma = pltpu.SemaphoreType.DMA
-    loss, gq, gd = pl.pallas_call(
+    loss, accq, accd, inq, ind = pl.pallas_call(
         kernel,
-        out_shape=(jax.ShapeDtypeStruct((1, N), f32),
+        out_shape=(jax.ShapeDtypeStruct((N,), f32),
                    jax.ShapeDtypeStruct((N, E), f32),
-                   jax.ShapeDtypeStruct((N, E), f32)),
-        in_specs=[pl.BlockSpec(memory_space=pl.ANY), pl.BlockSpec(memory_space=pl.ANY),
+                   jax.ShapeDtypeStruct((N, E), f32),
+                   jax.ShapeDtypeStruct((2, N, E), bf16),
+                   jax.ShapeDtypeStruct((2, N, E), bf16)),
+        in_specs=[pl.BlockSpec(memory_space=pltpu.HBM), pl.BlockSpec(memory_space=pltpu.HBM),
                   pl.BlockSpec(memory_space=pltpu.VMEM)],
-        out_specs=(pl.BlockSpec(memory_space=pltpu.VMEM), pl.BlockSpec(memory_space=pl.ANY),
-                   pl.BlockSpec(memory_space=pl.ANY)),
+        out_specs=(pl.BlockSpec(memory_space=pltpu.VMEM),) + (pl.BlockSpec(memory_space=pl.ANY),) * 4,
         scratch_shapes=[
             pltpu.VMEM((W3, E), bf16), pltpu.VMEM((W3, E), bf16),
             pltpu.VMEM((2, W3, W3), f32), pltpu.VMEM((2, W3, W3), bf16),
             pltpu.VMEM((2, W3, 128), f32),
             pltpu.VMEM((2, 1, W3), f32), pltpu.VMEM((2, 4, 1, W3), f32), pltpu.VMEM((2, 1, W3), f32),
-            pltpu.VMEM((2, 2 * N, E), bf16), pltpu.VMEM((2, 2 * N, E), bf16), pltpu.VMEM((2, 2 * N, E), bf16),
+            pltpu.VMEM((2, 2 * N, E), bf16), pltpu.VMEM((2, 2 * N, E), bf16),
             pltpu.VMEM((2, N, E), f32),
             dma((2,)), dma((2, 4)), dma((2, 4)),
             dma((2, 2, C)), dma((2, 2, C)), dma((2, 2, C)), dma((2, 2, C)), dma((2, 2, C)),
-            dma((2, 2, C)), dma((2, 2, C)), dma((2, C)),
+            dma((2, 2, C)), dma((2, 2, C)), dma((2,)), dma((2, 2)),
         ],
         compiler_params=pltpu.CompilerParams(
             collective_id=0, has_side_effects=True, vmem_limit_bytes=60 * 1024 * 1024),
         cost_estimate=pl.CostEstimate(flops=11_000_000_000, bytes_accessed=8_000_000,
                                       transcendentals=11_000_000),
-    )(queries, documents, positives.reshape(1, N))
-    return loss.reshape(N), gq, gd
+    )(queries, documents, positives)
+
+    def total(a, x):
+        return LOGIT_SCALE * (a + x[0].astype(f32) + x[1].astype(f32))
+
+    return loss, total(accq, inq), total(accd, ind)
 
 
 def solution(mesh):

time: 194 us -> 192 us (0.990)
  the two profiles are of different devices: /device:TPU:58 before, /device:TPU:5 now
where the time goes in v3:
time: 192 us
  Pallas kernels  185 us (96%)
  other arithmetic  5.39 us (3%)
    pallas_call x1, Pallas kernels, per_device(): pl.pallas_call(kernel, out_shape=(jax.ShapeDtypeStruct((N,), f32), jax.Sh...  185 us
    mul x1, other arithmetic, total(): return LOGIT_SCALE * (a + x[0].astype(f32) + x[1].astype(f32))  5.39 us

profile of v3, /device:TPU:5, one launch (start us, length us, event | category | flops | bytes accessed | tf_op | source)
XLA Modules:
  0.0 192.1 jit_solution(13283876252139068373)
XLA Ops:
  0.6 185.5 %shard_map.58 = (f32[384]{0:T(512)}, f32[384,1024]{1,0:T(8,128)}, f32[384,1024]{1,0:T(8,128)}, bf16[2,384,1024]{2,1,0:T(8,128)(2,1)}, bf16[2,384,1024]{2,1,0:T(8,128)(2,1)}) custom-call(bf16[384,1024]{1,0:T(8,128)(2,1)} %q_ref.1, bf16[384,1024]{1,0:T(8,128)(2,1)} %d_ref.1, s32[384]{0:T(512)} %p_ref.1), custom_call_target="tpu_custom_call" | custom-call | flops 11000000512 | bytes 8000000 | tf_op jit(solution)/shard_map/pallas_call | solution.py:330
  186.1 0.0 copy-start
  186.1 5.4 %fusion = (f32[384,1024]{1,0:T(8,128)}, f32[384,1024]{1,0:T(8,128)}) fusion(f32[384,1024]{1,0:T(8,128)} %get-tuple-element.11, bf16[2,384,1024]{2,1,0:T(8,128)(2,1)} %get-tuple-element.12, bf16[2,384,1024]{2,1,0:T(8,128)(2,1)} %get-tuple-element.10, f32[384,1024]{1,0:T(8,128)} %get-tuple-element.9), kind=kLoop, calls=%fused_computation.1 | loop fusion | flops 3932160 | bytes 9437184 | tf_op jit(solution)/shard_map/mul | solution.py:358
  191.5 0.0 copy-done
  191.5 0.6 copy.7
Async XLA Ops:
  186.1 5.4 %copy-start = (f32[384]{0:T(512)S(1)}, f32[384]{0:T(512)}, u32[]{:S(2)}) copy-start(f32[384]{0:T(512)} %get-tuple-element.18) | copy-start | bytes 4612

commit v4 on v3

--- a/solution.py
+++ b/solution.py
@@ -13,10 +13,11 @@
 C = 6
 R = N // C
 STRIP = 32
+SUM_ROWS = 48
 ORDER = ((1, 0), (1, 1), (0, 0), (0, 1), (1, 2), (1, 3), (0, 2), (0, 3), (1, 4), (1, 5), (0, 4), (0, 5))
 OFFS = (1, 3)
-FWD_MODES = ((8584, 130, 70, 33, 38937, 38937, 33792, 514), (27206, 41494, 10256, 10400, 34833, 10256, 33045, 32788))
-BACK_MODES = ((16512, 0, 512, 96, 34840, 4113, 1024, 4), (32833, 43521, 2180, 8577, 2321, 2194, 42244, 16))
+FWD_MODES = ((16768, 4480, 69, 33, 38937, 38929, 33792, 512), (26693, 41558, 10257, 10625, 2064, 10260, 1300, 20))
+BACK_MODES = ((0, 10, 8192, 64, 32776, 4097, 512, 0), (32833, 33281, 2048, 8321, 2064, 2064, 33028, 16))
 
 
 def spot(q, plus):
@@ -231,8 +232,8 @@
             def _():
                 zero_side(k, plus).wait()
 
-    for k in (1, 0):
-        for j in range(3):
+    for j in range(3):
+        for k in (1, 0):
             weights(k, N + 256 * j, N + 256 * j + 256)
             product(k, N + 256 * j, 256, outb.at[k], 256 * j)
             for q in (2 * j, 2 * j + 1):
@@ -256,6 +257,7 @@
                 give(k, plus, q).start()
 
     relay_back(1, 0)
+    relay_back(0, 0)
     weights(1, 0, N)
     weights(0, 0, N)
     pos = lax.rem(p_ref[...].reshape(1, N), N)
@@ -266,6 +268,7 @@
     col_at = jnp.sum(jnp.where(hit, lcol[1, 0:N, 0:1], 0.0), axis=0, keepdims=True)
     loss_ref[...] = (0.5 * (full[1, :, 0:N] - score_at) + 0.5 * (col_at - score_at)).reshape(loss_ref.shape)
     relay_back(1, 1)
+    relay_back(0, 1)
 
     @pl.loop(0, N // STRIP)
     def _(i):
@@ -279,19 +282,21 @@
             w[g, rows, 0:N] = (v - match.astype(jnp.float32)).astype(jnp.bfloat16)
 
     relay_back(1, 2)
+    relay_back(0, 2)
     product(0, 0, N, acc.at[0], 0)
     relay_back(1, 3)
+    relay_back(0, 3)
     product(1, 0, N, acc.at[1], 0)
     relay_back(1, 4)
+    relay_back(0, 4)
     relay_back(1, 5)
-    for q in range(C):
-        relay_back(0, q)
+    relay_back(0, 5)
 
     outs = [pltpu.make_async_copy(acc.at[k], (accq_ref, accd_ref)[k], o_sem.at[k]) for k in (0, 1)]
     for cp in outs:
         cp.start()
-    for k in (1, 0):
-        for q in range(C):
+    for q in range(C):
+        for k in (1, 0):
             @pl.when(bmode[k][2] != 1)
             def _():
                 give(k, 1, q).wait_recv()
@@ -322,6 +327,12 @@
         cp.wait_send()
     for cp in outs:
         cp.wait()
+
+
+def sum_kernel(loss_in, aq, ad, xq, xd, loss_out, gq, gd):
+    loss_out[...] = loss_in[...]
+    for a, x, g in ((aq, xq, gq), (ad, xd, gd)):
+        g[...] = LOGIT_SCALE * (a[...] + x[0].astype(jnp.float32) + x[1].astype(jnp.float32))
 
 
 def per_device(queries, documents, positives):
@@ -354,10 +365,19 @@
                                       transcendentals=11_000_000),
     )(queries, documents, positives)
 
-    def total(a, x):
-        return LOGIT_SCALE * (a + x[0].astype(f32) + x[1].astype(f32))
-
-    return loss, total(accq, inq), total(accd, ind)
+    rows = pl.BlockSpec((SUM_ROWS, E), lambda i: (i, 0))
+    both = pl.BlockSpec((2, SUM_ROWS, E), lambda i: (0, i, 0))
+    whole = pl.BlockSpec((N,), lambda i: (0,))
+    return pl.pallas_call(
+        sum_kernel,
+        grid=(N // SUM_ROWS,),
+        out_shape=(jax.ShapeDtypeStruct((N,), f32),
+                   jax.ShapeDtypeStruct((N, E), f32),
+                   jax.ShapeDtypeStruct((N, E), f32)),
+        in_specs=[whole, rows, rows, both, both],
+        out_specs=(whole, rows, rows),
+        compiler_params=pltpu.CompilerParams(vmem_limit_bytes=60 * 1024 * 1024),
+    )(loss, accq, accd, inq, ind)
 
 
 def solution(mesh):

time: 192 us -> 189 us (0.984)
  the two profiles are of different devices: /device:TPU:5 before, /device:TPU:1 now
where the time goes in v4:
time: 189 us
  Pallas kernels  188 us (99%)
    pallas_call x1, Pallas kernels, per_device(): pl.pallas_call(kernel, out_shape=(jax.ShapeDtypeStruct((N,), f32), jax.Sh...  181 us
    pallas_call x1, Pallas kernels, per_device(): pl.pallas_call(sum_kernel, grid=(N // SUM_ROWS,), out_shape=(jax.ShapeDty...  6.79 us

profile of v4, /device:TPU:1, one launch (start us, length us, event | category | flops | bytes accessed | tf_op | source)
XLA Modules:
  0.0 188.8 jit_solution(180231260083943589)
XLA Ops:
  0.6 181.3 %shard_map.58 = (f32[384]{0:T(512)}, f32[384,1024]{1,0:T(8,128)}, f32[384,1024]{1,0:T(8,128)}, bf16[2,384,1024]{2,1,0:T(8,128)(2,1)}, bf16[2,384,1024]{2,1,0:T(8,128)(2,1)}) custom-call(bf16[384,1024]{1,0:T(8,128)(2,1)} %q_ref.1, bf16[384,1024]{1,0:T(8,128)(2,1)} %d_ref.1, s32[384]{0:T(512)} %p_ref.1), custom_call_target="tpu_custom_call" | custom-call | flops 11000000512 | bytes 8000000 | tf_op jit(solution)/shard_map/pallas_call | solution.py:341
  182.0 6.8 %shard_map.59 = (f32[384]{0:T(512)}, f32[384,1024]{1,0:T(8,128)}, f32[384,1024]{1,0:T(8,128)}) custom-call(f32[384]{0:T(512)} %get-tuple-element.8.loss_in, f32[384,1024]{1,0:T(8,128)} %get-tuple-element.9.aq, f32[384,1024]{1,0:T(8,128)} %get-tuple-element.10.ad, bf16[2,384,1024]{2,1,0:T(8,128)(2,1)} %get-tuple-element.11.xq, ...), custom_call_target="tpu_custom_call" | custom-call | tf_op jit(solution)/shard_map/pallas_call | solution.py:371

commit v5 on v3

--- a/solution.py
+++ b/solution.py
@@ -10,27 +10,28 @@
 N = 384
 E = 1024
 W3 = 3 * N
-C = 6
+C = 12
 R = N // C
+Q3 = C // 3
 STRIP = 32
-ORDER = ((1, 0), (1, 1), (0, 0), (0, 1), (1, 2), (1, 3), (0, 2), (0, 3), (1, 4), (1, 5), (0, 4), (0, 5))
+ORDER = tuple((1, q) for q in range(Q3 // 2)) + tuple(
+    x for q in range(C) for x in (((1, q + Q3 // 2),) if q + Q3 // 2 < C else ()) + ((0, q),))
 OFFS = (1, 3)
-FWD_MODES = ((8584, 130, 70, 33, 38937, 38937, 33792, 514), (27206, 41494, 10256, 10400, 34833, 10256, 33045, 32788))
-BACK_MODES = ((16512, 0, 512, 96, 34840, 4113, 1024, 4), (32833, 43521, 2180, 8577, 2321, 2194, 42244, 16))
+FWD_MODES = ((16768, 4480, 69, 33, 38937, 38929, 33792, 512), (26693, 41558, 10257, 10625, 2064, 10260, 1300, 20))
+BACK_MODES = ((0, 10, 8192, 64, 32776, 4097, 512, 0), (32833, 33281, 2048, 8321, 2064, 2064, 33028, 16))
 
 
 def spot(q, plus):
-    return (q // 2) * 4 * R + plus * 2 * R + (q % 2) * R
-
-
-def kernel(q_ref, d_ref, p_ref, loss_ref, accq_ref, accd_ref, inq_ref, ind_ref,
-           qc, dc, s, w, lcol, part, got, full, outb, rel, acc,
-           loc_sem, lse_ssem, lse_rsem, f_ssem, f_rsem, g_ssem, b_ssem, b_rsem, r_ssem, r_rsem, o_sem, z_sem):
+    return (q // Q3) * 256 + plus * 128 + (q % Q3) * R
+
+
+def kernel(q_ref, d_ref, p_ref, loss_ref, gq_ref, gd_ref,
+           qc, dc, s, w, lcol, part, got, full, outb, inb, rel, acc,
+           loc_sem, lse_ssem, lse_rsem, f_ssem, f_rsem, g_ssem, b_ssem, b_rsem, r_ssem, r_rsem, o_sem):
     me = lax.axis_index("dx") * 16 + lax.axis_index("dy")
     ring = lax.rem(me * 241, 256)
     cat = (qc, dc)
     src = (q_ref, d_ref)
-    inb = (inq_ref, ind_ref)
 
     def dev(o):
         k = lax.rem(me + (17 * o) % 256, 256)
@@ -140,27 +141,16 @@
         part[g, :, 0:n] = y
         part[1 - g, :, r0:r1] = log_sum(1 - g, 0, n, r0, r1)
 
-    outb[0, 0:N, :] = jnp.zeros((N, E), jnp.bfloat16)
-
-    def zero_side(k, plus):
-        return pltpu.make_async_copy(outb.at[0, pl.ds(0, N)], inb[k].at[plus], z_sem.at[k, plus])
-
-    for k in (0, 1):
-        for plus in (0, 1):
-            @pl.when(bmode[k][2] == 1 + plus)
-            def _():
-                zero_side(k, plus).start()
-
     append(0, 0, N, N)
-    plan = sorted([(i, 0, k, q) for i, (k, q) in enumerate(ORDER)] + [(i + 3, 1, k, q) for i, (k, q) in enumerate(ORDER)])
+    plan = sorted([(i, 0, k, q) for i, (k, q) in enumerate(ORDER)] + [(i + 5, 1, k, q) for i, (k, q) in enumerate(ORDER)])
     for _, late, k, q in plan:
         if not late:
             pass_on(k, q)
         else:
             take(k, q)
-            if q % 2 == 1:
-                base = N + (q // 2) * 4 * R
-                append(k, base, base + 4 * R, base + (4 * R if k == 0 else 0))
+            if q % Q3 == Q3 - 1:
+                base = N + (q // Q3) * 256
+                append(k, base, base + 256, base + (256 if k == 0 else 0))
 
     lse_copies = []
     for g in (0, 1):
@@ -208,7 +198,7 @@
 
     def give(k, plus, q):
         o = OFFS[k] if plus == 1 else -OFFS[k]
-        return rcopy(outb.at[k, pl.ds(spot(q, plus), R)], inb[k].at[1 - plus, pl.ds(q * R, R)],
+        return rcopy(outb.at[k, pl.ds(spot(q, plus), R)], inb.at[k, 1 - plus, pl.ds(q * R, R)],
                      b_ssem.at[k, plus, q], b_rsem.at[k, 1 - plus, q], o)
 
     def lend(k, plus, q):
@@ -225,17 +215,11 @@
     def is_relay(k, plus):
         return bmode[k][plus] == (2 if plus == 1 else 1)
 
-    for k in (0, 1):
-        for plus in (0, 1):
-            @pl.when(bmode[k][2] == 1 + plus)
-            def _():
-                zero_side(k, plus).wait()
-
-    for k in (1, 0):
-        for j in range(3):
+    for j in range(3):
+        for k in (1, 0):
             weights(k, N + 256 * j, N + 256 * j + 256)
             product(k, N + 256 * j, 256, outb.at[k], 256 * j)
-            for q in (2 * j, 2 * j + 1):
+            for q in range(Q3 * j, Q3 * j + Q3):
                 for plus in (0, 1):
                     @pl.when(is_leaf(k, plus))
                     def _():
@@ -255,7 +239,12 @@
                                     + rel[k, rows, :].astype(jnp.float32)).astype(jnp.bfloat16)
                 give(k, plus, q).start()
 
-    relay_back(1, 0)
+    def relay_two(i):
+        for q in (2 * i, 2 * i + 1):
+            for k in (1, 0):
+                relay_back(k, q)
+
+    relay_two(0)
     weights(1, 0, N)
     weights(0, 0, N)
     pos = lax.rem(p_ref[...].reshape(1, N), N)
@@ -265,7 +254,7 @@
     score_at = jnp.sum(jnp.where(hit, x, 0.0), axis=0, keepdims=True)
     col_at = jnp.sum(jnp.where(hit, lcol[1, 0:N, 0:1], 0.0), axis=0, keepdims=True)
     loss_ref[...] = (0.5 * (full[1, :, 0:N] - score_at) + 0.5 * (col_at - score_at)).reshape(loss_ref.shape)
-    relay_back(1, 1)
+    relay_two(1)
 
     @pl.loop(0, N // STRIP)
     def _(i):
@@ -278,27 +267,32 @@
             v = 0.5 * (jnp.exp(x - lcol[g, rows, 0:1]) + jnp.exp(x - full[g, :, 0:N]))
             w[g, rows, 0:N] = (v - match.astype(jnp.float32)).astype(jnp.bfloat16)
 
-    relay_back(1, 2)
+    relay_two(2)
     product(0, 0, N, acc.at[0], 0)
-    relay_back(1, 3)
+    relay_two(3)
     product(1, 0, N, acc.at[1], 0)
-    relay_back(1, 4)
-    relay_back(1, 5)
+    relay_two(4)
+    relay_two(5)
+
+    outs = []
     for q in range(C):
-        relay_back(0, q)
-
-    outs = [pltpu.make_async_copy(acc.at[k], (accq_ref, accd_ref)[k], o_sem.at[k]) for k in (0, 1)]
-    for cp in outs:
-        cp.start()
-    for k in (1, 0):
-        for q in range(C):
+        for k, res in ((1, gd_ref), (0, gq_ref)):
+            rows = pl.ds(q * R, R)
+
             @pl.when(bmode[k][2] != 1)
             def _():
                 give(k, 1, q).wait_recv()
+                acc[k, rows, :] = acc[k, rows, :] + inb[k, 0, rows, :].astype(jnp.float32)
 
             @pl.when(bmode[k][2] != 2)
             def _():
                 give(k, 0, q).wait_recv()
+                acc[k, rows, :] = acc[k, rows, :] + inb[k, 1, rows, :].astype(jnp.float32)
+
+            acc[k, rows, :] = LOGIT_SCALE * acc[k, rows, :]
+            cp = pltpu.make_async_copy(acc.at[k, rows], res.at[rows], o_sem.at[k, q])
+            cp.start()
+            outs.append(cp)
 
     for k in (0, 1):
         for q in range(C):
@@ -327,37 +321,30 @@
 def per_device(queries, documents, positives):
     f32, bf16 = jnp.float32, jnp.bfloat16
     dma = pltpu.SemaphoreType.DMA
-    loss, accq, accd, inq, ind = pl.pallas_call(
+    return pl.pallas_call(
         kernel,
         out_shape=(jax.ShapeDtypeStruct((N,), f32),
                    jax.ShapeDtypeStruct((N, E), f32),
-                   jax.ShapeDtypeStruct((N, E), f32),
-                   jax.ShapeDtypeStruct((2, N, E), bf16),
-                   jax.ShapeDtypeStruct((2, N, E), bf16)),
+                   jax.ShapeDtypeStruct((N, E), f32)),
         in_specs=[pl.BlockSpec(memory_space=pltpu.HBM), pl.BlockSpec(memory_space=pltpu.HBM),
                   pl.BlockSpec(memory_space=pltpu.VMEM)],
-        out_specs=(pl.BlockSpec(memory_space=pltpu.VMEM),) + (pl.BlockSpec(memory_space=pl.ANY),) * 4,
+        out_specs=(pl.BlockSpec(memory_space=pltpu.VMEM),) + (pl.BlockSpec(memory_space=pl.ANY),) * 2,
         scratch_shapes=[
             pltpu.VMEM((W3, E), bf16), pltpu.VMEM((W3, E), bf16),
             pltpu.VMEM((2, W3, W3), f32), pltpu.VMEM((2, W3, W3), bf16),
             pltpu.VMEM((2, W3, 128), f32),
             pltpu.VMEM((2, 1, W3), f32), pltpu.VMEM((2, 4, 1, W3), f32), pltpu.VMEM((2, 1, W3), f32),
-            pltpu.VMEM((2, 2 * N, E), bf16), pltpu.VMEM((2, 2 * N, E), bf16),
+            pltpu.VMEM((2, 2 * N, E), bf16), pltpu.VMEM((2, 2, N, E), bf16), pltpu.VMEM((2, 2 * N, E), bf16),
             pltpu.VMEM((2, N, E), f32),
             dma((2,)), dma((2, 4)), dma((2, 4)),
             dma((2, 2, C)), dma((2, 2, C)), dma((2, 2, C)), dma((2, 2, C)), dma((2, 2, C)),
-            dma((2, 2, C)), dma((2, 2, C)), dma((2,)), dma((2, 2)),
+            dma((2, 2, C)), dma((2, 2, C)), dma((2, C)),
         ],
         compiler_params=pltpu.CompilerParams(
             collective_id=0, has_side_effects=True, vmem_limit_bytes=60 * 1024 * 1024),
         cost_estimate=pl.CostEstimate(flops=11_000_000_000, bytes_accessed=8_000_000,
                                       transcendentals=11_000_000),
     )(queries, documents, positives)
-
-    def total(a, x):
-        return LOGIT_SCALE * (a + x[0].astype(f32) + x[1].astype(f32))
-
-    return loss, total(accq, inq), total(accd, ind)
 
 
 def solution(mesh):

time: 192 us -> 190 us (0.990)
  the two profiles are of different devices: /device:TPU:5 before, /device:TPU:1 now
where the time goes in v5:
time: 190 us
  Pallas kernels  184 us (97%)
  local copies, waits for them, and re-layouts  5.25 us (3%)
    pallas_call x1, Pallas kernels, per_device(): pl.pallas_call(kernel, out_shape=(jax.ShapeDtypeStruct((N,), f32), jax.Sh...  184 us
    unnamed x5, local copies, waits for them, and re-layouts  5.25 us

profile of v5, /device:TPU:1, one launch (start us, length us, event | category | flops | bytes accessed | tf_op | source)
XLA Modules:
  0.0 189.7 jit_solution(2192459929346163636)
XLA Ops:
  0.6 183.8 %shard_map.58 = (f32[384]{0:T(512)}, f32[384,1024]{1,0:T(8,128)}, f32[384,1024]{1,0:T(8,128)}) custom-call(bf16[384,1024]{1,0:T(8,128)(2,1)} %q_ref.1, bf16[384,1024]{1,0:T(8,128)(2,1)} %d_ref.1, s32[384]{0:T(512)} %p_ref.1), custom_call_target="tpu_custom_call" | custom-call | flops 11000000512 | bytes 8000000 | tf_op jit(solution)/shard_map/pallas_call | solution.py:324
  184.5 1.3 copy.9
  185.7 0.0 copy-start
  185.7 2.8 %copy.10 = f32[384,1024]{1,0:T(8,128)} copy(f32[384,1024]{1,0:T(8,128)} %get-tuple-element.7) | data formatting | bytes 3145728
  188.6 0.0 copy-done
  188.6 1.1 copy.11
Async XLA Ops:
  185.7 2.9 %copy-start = (f32[384,1024]{1,0:T(8,128)S(1)}, f32[384,1024]{1,0:T(8,128)}, u32[]{:S(2)}) copy-start(f32[384,1024]{1,0:T(8,128)} %get-tuple-element.8) | copy-start | bytes 4718596

commit v6 on v5

--- a/solution.py
+++ b/solution.py
@@ -10,15 +10,18 @@
 N = 384
 E = 1024
 W3 = 3 * N
-C = 12
+C = 6
 R = N // C
 Q3 = C // 3
 STRIP = 32
 ORDER = tuple((1, q) for q in range(Q3 // 2)) + tuple(
     x for q in range(C) for x in (((1, q + Q3 // 2),) if q + Q3 // 2 < C else ()) + ((0, q),))
 OFFS = (1, 3)
-FWD_MODES = ((16768, 4480, 69, 33, 38937, 38929, 33792, 512), (26693, 41558, 10257, 10625, 2064, 10260, 1300, 20))
-BACK_MODES = ((0, 10, 8192, 64, 32776, 4097, 512, 0), (32833, 33281, 2048, 8321, 2064, 2064, 33028, 16))
+FWD_MODES = (
+    ((0, 0, 64, 1129, 32808, 39429, 17936, 1536), (27205, 41556, 10641, 43137, 33829, 43030, 34073, 34836)),
+    ((0, 2304, 2088, 33, 32897, 32785, 41984, 16896), (65, 33090, 2065, 10369, 34912, 10337, 33060, 32784)),
+)
+BACK_MODES = ((0, 0, 0, 0, 34824, 4105, 1024, 0), (32833, 35329, 2052, 8321, 2064, 2064, 33028, 16))
 
 
 def spot(q, plus):
@@ -60,7 +63,7 @@
     barrier = pltpu.get_barrier_semaphore()
     for o in (1, -1, 2, -2, 3, -3, 6, -6):
         pl.semaphore_signal(barrier, inc=1, device_id=dev(o), device_id_type=MESH)
-    fmode = [[mode_of(FWD_MODES[k], d * OFFS[k]) for d in (-1, 1, 0)] for k in (0, 1)]
+    fmode = [[[mode_of(FWD_MODES[h][k], d * OFFS[k]) for d in (-1, 1, 0)] for k in (0, 1)] for h in (0, 1)]
     bmode = [[mode_of(BACK_MODES[k], d * OFFS[k]) for d in (-1, 1, 0)] for k in (0, 1)]
     pl.semaphore_wait(barrier, 8)
 
@@ -77,28 +80,28 @@
         return rcopy(slot(k, plus, q), slot(k, 1 - plus, q),
                      g_ssem.at[k, plus, q], f_rsem.at[k, 1 - plus, q], o)
 
-    def relays(k, plus):
-        return fmode[k][plus] == (1 if plus == 0 else 2)
-
-    def sends_to(k, plus):
-        return fmode[k][2] != (2 if plus == 0 else 1)
+    def relays(k, plus, q):
+        return fmode[2 * q // C][k][plus] == (1 if plus == 0 else 2)
+
+    def sends_to(k, plus, q):
+        return fmode[2 * q // C][k][2] != (2 if plus == 0 else 1)
 
     for k, q in ORDER:
         for plus in (0, 1):
-            @pl.when(sends_to(k, plus))
+            @pl.when(sends_to(k, plus, q))
             def _():
                 send(k, plus, q).start()
 
     def pass_on(k, q):
         for plus in (0, 1):
-            @pl.when(relays(k, plus))
+            @pl.when(relays(k, plus, q))
             def _():
                 send(k, plus, q).wait_recv()
                 forward(k, plus, q).start()
 
     def take(k, q):
         for plus in (0, 1):
-            @pl.when(jnp.logical_not(relays(k, plus)))
+            @pl.when(jnp.logical_not(relays(k, plus, q)))
             def _():
                 send(k, plus, q).wait_recv()
 
@@ -112,19 +115,20 @@
 
     def log_sum(g, r0, r1, c0, c1):
         n = c1 - c0
-        steps = (r1 - r0) // STRIP
+        tall = 128 if n <= 256 else 64 if n <= 640 else STRIP
+        steps = (r1 - r0) // tall
 
         def strip(i):
-            return s[g, pl.ds(pl.multiple_of(r0 + i * STRIP, STRIP), STRIP), c0:c1]
+            return s[g, pl.ds(pl.multiple_of(r0 + i * tall, tall), tall), c0:c1]
 
         def top(i, m):
-            return jnp.maximum(m, jnp.max(strip(i).reshape(STRIP // 8, 8, n), axis=0))
+            return jnp.maximum(m, jnp.max(strip(i).reshape(tall // 8, 8, n), axis=0))
 
         m = lax.fori_loop(0, steps, top, jnp.full((8, n), -jnp.inf, jnp.float32))
         m = jnp.max(m, axis=0, keepdims=True)
 
         def add(i, t):
-            return t + jnp.sum(jnp.exp(strip(i) - m).reshape(STRIP // 8, 8, n), axis=0)
+            return t + jnp.sum(jnp.exp(strip(i) - m).reshape(tall // 8, 8, n), axis=0)
 
         t = lax.fori_loop(0, steps, add, jnp.zeros((8, n), jnp.float32))
         return m + jnp.log(jnp.sum(t, axis=0, keepdims=True))
@@ -142,7 +146,7 @@
         part[1 - g, :, r0:r1] = log_sum(1 - g, 0, n, r0, r1)
 
     append(0, 0, N, N)
-    plan = sorted([(i, 0, k, q) for i, (k, q) in enumerate(ORDER)] + [(i + 5, 1, k, q) for i, (k, q) in enumerate(ORDER)])
+    plan = sorted([(i, 0, k, q) for i, (k, q) in enumerate(ORDER)] + [(i + 3, 1, k, q) for i, (k, q) in enumerate(ORDER)])
     for _, late, k, q in plan:
         if not late:
             pass_on(k, q)
@@ -239,12 +243,11 @@
                                     + rel[k, rows, :].astype(jnp.float32)).astype(jnp.bfloat16)
                 give(k, plus, q).start()
 
-    def relay_two(i):
-        for q in (2 * i, 2 * i + 1):
-            for k in (1, 0):
-                relay_back(k, q)
-
-    relay_two(0)
+    def relay_both(q):
+        for k in (1, 0):
+            relay_back(k, q)
+
+    relay_both(0)
     weights(1, 0, N)
     weights(0, 0, N)
     pos = lax.rem(p_ref[...].reshape(1, N), N)
@@ -254,7 +257,7 @@
     score_at = jnp.sum(jnp.where(hit, x, 0.0), axis=0, keepdims=True)
     col_at = jnp.sum(jnp.where(hit, lcol[1, 0:N, 0:1], 0.0), axis=0, keepdims=True)
     loss_ref[...] = (0.5 * (full[1, :, 0:N] - score_at) + 0.5 * (col_at - score_at)).reshape(loss_ref.shape)
-    relay_two(1)
+    relay_both(1)
 
     @pl.loop(0, N // STRIP)
     def _(i):
@@ -267,12 +270,12 @@
             v = 0.5 * (jnp.exp(x - lcol[g, rows, 0:1]) + jnp.exp(x - full[g, :, 0:N]))
             w[g, rows, 0:N] = (v - match.astype(jnp.float32)).astype(jnp.bfloat16)
 
-    relay_two(2)
+    relay_both(2)
     product(0, 0, N, acc.at[0], 0)
-    relay_two(3)
+    relay_both(3)
     product(1, 0, N, acc.at[1], 0)
-    relay_two(4)
-    relay_two(5)
+    relay_both(4)
+    relay_both(5)
 
     outs = []
     for q in range(C):
@@ -297,11 +300,11 @@
     for k in (0, 1):
         for q in range(C):
             for plus in (0, 1):
-                @pl.when(sends_to(k, plus))
+                @pl.when(sends_to(k, plus, q))
                 def _():
                     send(k, plus, q).wait_send()
 
-                @pl.when(relays(k, plus))
+                @pl.when(relays(k, plus, q))
                 def _():
                     forward(k, plus, q).wait_send()
 

time: 190 us -> 195 us (1.026)
  Pallas kernels: 184 us -> 189 us
    pallas_call x1, Pallas kernels: 184 us -> 189 us  [per_device(): pl.pallas_call(kernel, out_shape=(jax.ShapeDtypeStruct((N,), f32), jax.Sh...]
where the time goes in v6:
time: 195 us
  Pallas kernels  189 us (97%)
  local copies, waits for them, and re-layouts  5.25 us (3%)
    pallas_call x1, Pallas kernels, per_device(): pl.pallas_call(kernel, out_shape=(jax.ShapeDtypeStruct((N,), f32), jax.Sh...  189 us
    unnamed x5, local copies, waits for them, and re-layouts  5.25 us

profile of v6, /device:TPU:1, one launch (start us, length us, event | category | flops | bytes accessed | tf_op | source)
XLA Modules:
  0.0 195.1 jit_solution(3918460526007337937)
XLA Ops:
  0.6 189.2 %shard_map.58 = (f32[384]{0:T(512)}, f32[384,1024]{1,0:T(8,128)}, f32[384,1024]{1,0:T(8,128)}) custom-call(bf16[384,1024]{1,0:T(8,128)(2,1)} %q_ref.1, bf16[384,1024]{1,0:T(8,128)(2,1)} %d_ref.1, s32[384]{0:T(512)} %p_ref.1), custom_call_target="tpu_custom_call" | custom-call | flops 11000000512 | bytes 8000000 | tf_op jit(solution)/shard_map/pallas_call | solution.py:327
  189.8 1.3 copy.9
  191.1 0.0 copy-start
  191.1 2.8 %copy.10 = f32[384,1024]{1,0:T(8,128)} copy(f32[384,1024]{1,0:T(8,128)} %get-tuple-element.7) | data formatting | bytes 3145728
  194.0 0.0 copy-done
  194.0 1.1 copy.11
Async XLA Ops:
  191.1 2.9 %copy-start = (f32[384,1024]{1,0:T(8,128)S(1)}, f32[384,1024]{1,0:T(8,128)}, u32[]{:S(2)}) copy-start(f32[384,1024]{1,0:T(8,128)} %get-tuple-element.8) | copy-start | bytes 4718596

commit v7 on v6

--- a/solution.py
+++ b/solution.py
@@ -14,14 +14,10 @@
 R = N // C
 Q3 = C // 3
 STRIP = 32
-ORDER = tuple((1, q) for q in range(Q3 // 2)) + tuple(
-    x for q in range(C) for x in (((1, q + Q3 // 2),) if q + Q3 // 2 < C else ()) + ((0, q),))
+ORDER = ((1, 0), (1, 1), (0, 0), (0, 1), (1, 2), (1, 3), (0, 2), (0, 3), (1, 4), (1, 5), (0, 4), (0, 5))
 OFFS = (1, 3)
-FWD_MODES = (
-    ((0, 0, 64, 1129, 32808, 39429, 17936, 1536), (27205, 41556, 10641, 43137, 33829, 43030, 34073, 34836)),
-    ((0, 2304, 2088, 33, 32897, 32785, 41984, 16896), (65, 33090, 2065, 10369, 34912, 10337, 33060, 32784)),
-)
-BACK_MODES = ((0, 0, 0, 0, 34824, 4105, 1024, 0), (32833, 35329, 2052, 8321, 2064, 2064, 33028, 16))
+FWD_MODES = ((0, 0, 96, 32, 32784, 1, 0, 1536), (10821, 43076, 8209, 43169, 1045, 43040, 1045, 34820))
+BACK_MODES = ((0, 128, 32768, 0, 16402, 18434, 8, 0), (22805, 41090, 8337, 43013, 34837, 43025, 21, 43012))
 
 
 def spot(q, plus):
@@ -63,7 +59,7 @@
     barrier = pltpu.get_barrier_semaphore()
     for o in (1, -1, 2, -2, 3, -3, 6, -6):
         pl.semaphore_signal(barrier, inc=1, device_id=dev(o), device_id_type=MESH)
-    fmode = [[[mode_of(FWD_MODES[h][k], d * OFFS[k]) for d in (-1, 1, 0)] for k in (0, 1)] for h in (0, 1)]
+    fmode = [[mode_of(FWD_MODES[k], d * OFFS[k]) for d in (-1, 1, 0)] for k in (0, 1)]
     bmode = [[mode_of(BACK_MODES[k], d * OFFS[k]) for d in (-1, 1, 0)] for k in (0, 1)]
     pl.semaphore_wait(barrier, 8)
 
@@ -80,28 +76,28 @@
         return rcopy(slot(k, plus, q), slot(k, 1 - plus, q),
                      g_ssem.at[k, plus, q], f_rsem.at[k, 1 - plus, q], o)
 
-    def relays(k, plus, q):
-        return fmode[2 * q // C][k][plus] == (1 if plus == 0 else 2)
-
-    def sends_to(k, plus, q):
-        return fmode[2 * q // C][k][2] != (2 if plus == 0 else 1)
+    def relays(k, plus):
+        return fmode[k][plus] == (1 if plus == 0 else 2)
+
+    def sends_to(k, plus):
+        return fmode[k][2] != (2 if plus == 0 else 1)
 
     for k, q in ORDER:
         for plus in (0, 1):
-            @pl.when(sends_to(k, plus, q))
+            @pl.when(sends_to(k, plus))
             def _():
                 send(k, plus, q).start()
 
     def pass_on(k, q):
         for plus in (0, 1):
-            @pl.when(relays(k, plus, q))
+            @pl.when(relays(k, plus))
             def _():
                 send(k, plus, q).wait_recv()
                 forward(k, plus, q).start()
 
     def take(k, q):
         for plus in (0, 1):
-            @pl.when(jnp.logical_not(relays(k, plus, q)))
+            @pl.when(jnp.logical_not(relays(k, plus)))
             def _():
                 send(k, plus, q).wait_recv()
 
@@ -300,11 +296,11 @@
     for k in (0, 1):
         for q in range(C):
             for plus in (0, 1):
-                @pl.when(sends_to(k, plus, q))
+                @pl.when(sends_to(k, plus))
                 def _():
                     send(k, plus, q).wait_send()
 
-                @pl.when(relays(k, plus, q))
+                @pl.when(relays(k, plus))
                 def _():
                     forward(k, plus, q).wait_send()
 

time: 195 us -> 185 us (0.949)
  Pallas kernels: 189 us -> 179 us
    pallas_call x1, Pallas kernels: 189 us -> 179 us  [per_device(): pl.pallas_call(kernel, out_shape=(jax.ShapeDtypeStruct((N,), f32), jax.Sh...]
where the time goes in v7:
time: 185 us
  Pallas kernels  179 us (97%)
  local copies, waits for them, and re-layouts  5.25 us (3%)
    pallas_call x1, Pallas kernels, per_device(): pl.pallas_call(kernel, out_shape=(jax.ShapeDtypeStruct((N,), f32), jax.Sh...  179 us
    unnamed x5, local copies, waits for them, and re-layouts  5.25 us

profile of v7, /device:TPU:1, one launch (start us, length us, event | category | flops | bytes accessed | tf_op | source)
XLA Modules:
  0.0 185.2 jit_solution(8987641454602508091)
XLA Ops:
  0.6 179.3 %shard_map.58 = (f32[384]{0:T(512)}, f32[384,1024]{1,0:T(8,128)}, f32[384,1024]{1,0:T(8,128)}) custom-call(bf16[384,1024]{1,0:T(8,128)(2,1)} %q_ref.1, bf16[384,1024]{1,0:T(8,128)(2,1)} %d_ref.1, s32[384]{0:T(512)} %p_ref.1), custom_call_target="tpu_custom_call" | custom-call | flops 11000000512 | bytes 8000000 | tf_op jit(solution)/shard_map/pallas_call | solution.py:323
  179.9 1.3 copy.9
  181.2 0.0 copy-start
  181.2 2.8 %copy.10 = f32[384,1024]{1,0:T(8,128)} copy(f32[384,1024]{1,0:T(8,128)} %get-tuple-element.7) | data formatting | bytes 3145728
  184.0 0.0 copy-done
  184.0 1.1 copy.11
Async XLA Ops:
  181.2 2.9 %copy-start = (f32[384,1024]{1,0:T(8,128)S(1)}, f32[384,1024]{1,0:T(8,128)}, u32[]{:S(2)}) copy-start(f32[384,1024]{1,0:T(8,128)} %get-tuple-element.8) | copy-start | bytes 4718596

commit v8 on v7

--- a/solution.py
+++ b/solution.py
@@ -17,7 +17,7 @@
 ORDER = ((1, 0), (1, 1), (0, 0), (0, 1), (1, 2), (1, 3), (0, 2), (0, 3), (1, 4), (1, 5), (0, 4), (0, 5))
 OFFS = (1, 3)
 FWD_MODES = ((0, 0, 96, 32, 32784, 1, 0, 1536), (10821, 43076, 8209, 43169, 1045, 43040, 1045, 34820))
-BACK_MODES = ((0, 128, 32768, 0, 16402, 18434, 8, 0), (22805, 41090, 8337, 43013, 34837, 43025, 21, 43012))
+BACK_MODES = ((0, 10, 8192, 64, 32776, 4097, 512, 0), (32833, 33281, 2048, 8321, 2064, 2064, 33028, 16))
 
 
 def spot(q, plus):

time: 185 us -> 179 us (0.968)
  Pallas kernels: 179 us -> 172 us
    pallas_call x1, Pallas kernels: 179 us -> 172 us  [per_device(): pl.pallas_call(kernel, out_shape=(jax.ShapeDtypeStruct((N,), f32), jax.Sh...]
where the time goes in v8:
time: 179 us; the launch traced here: 178 us
  Pallas kernels  172 us (96%)
  local copies, waits for them, and re-layouts  5.25 us (3%)
    pallas_call x1, Pallas kernels, per_device(): pl.pallas_call(kernel, out_shape=(jax.ShapeDtypeStruct((N,), f32), jax.Sh...  172 us
    unnamed x5, local copies, waits for them, and re-layouts  5.25 us

profile of v8, /device:TPU:1, one launch (start us, length us, event | category | flops | bytes accessed | tf_op | source)
XLA Modules:
  0.0 177.8 jit_solution(7217395179932961123)
XLA Ops:
  0.6 171.9 %shard_map.58 = (f32[384]{0:T(512)}, f32[384,1024]{1,0:T(8,128)}, f32[384,1024]{1,0:T(8,128)}) custom-call(bf16[384,1024]{1,0:T(8,128)(2,1)} %q_ref.1, bf16[384,1024]{1,0:T(8,128)(2,1)} %d_ref.1, s32[384]{0:T(512)} %p_ref.1), custom_call_target="tpu_custom_call" | custom-call | flops 11000000512 | bytes 8000000 | tf_op jit(solution)/shard_map/pallas_call | solution.py:323
  172.6 1.3 copy.9
  173.8 0.0 copy-start
  173.8 2.8 %copy.10 = f32[384,1024]{1,0:T(8,128)} copy(f32[384,1024]{1,0:T(8,128)} %get-tuple-element.7) | data formatting | bytes 3145728
  176.7 0.0 copy-done
  176.7 1.1 copy.11
Async XLA Ops:
  173.8 2.9 %copy-start = (f32[384,1024]{1,0:T(8,128)S(1)}, f32[384,1024]{1,0:T(8,128)}, u32[]{:S(2)}) copy-start(f32[384,1024]{1,0:T(8,128)} %get-tuple-element.8) | copy-start | bytes 4718596
